TPU v7x, 32 devices: a whole 2x2x4 slice. The times are simulated.
32 devices in a mesh: groups: 2 (over y), ctx: 4 (over z), state: 2 (over x), head: 2 (over core).
Axes of the slice: x: 2, y: 2, z: 4, core: 2. Of those that a mesh axis runs over, the one named last changes fastest.
Arguments:
- x_in: bfloat16 [4096, 4096], P(('groups', 'ctx'), 'head'), parts along dimension 0, may hold values from -6 to 6
- b_in: bfloat16 [4096, 1024], P(('groups', 'ctx'), 'state'), parts along dimension 0, may hold values from -6 to 6
- c_in: bfloat16 [4096, 1024], P(('groups', 'ctx'), 'state'), parts along dimension 0, may hold values from -6 to 6
- z_in: bfloat16 [4096, 4096], P(('groups', 'ctx'), ('head', 'state')), parts along dimension 0, may hold values from -6 to 6
- dt_raw: float32 [4096, 64], P(('groups', 'ctx'), 'head'), parts along dimension 0, may hold values from -5 to 5
- decay_rate: float32 [64], P('head'), may hold values from 0.00012207031 to 0.05, as said below
- d_skip: float32 [64], P('head'), may hold values from 0.5 to 1.5
- conv_x: float32 [4, 4096], P(None, 'head'), may hold values from -3 to 3
- conv_b: float32 [4, 1024], P(None, 'state'), may hold values from -0.3 to 0.3
- conv_c: float32 [4, 1024], P(None, 'state'), may hold values from -0.3 to 0.3
- norm_gain: float32 [4096], P(('head', 'state')), may hold values from 0.5 to 1.5
- w_out: bfloat16 [4096, 4096], P('ctx', ('state', 'head')), may hold values from -0.09375 to 0.09375
Outputs:
- layer_out: bfloat16 [4096, 4096], P(('groups', 'ctx'), ('state', 'head')), parts along dimension 0
There are 2 independent parts, one for each index of `groups`. A program takes and returns all parts, laid end to end along the dimension named above; an argument that names none is the same for every part. Nothing has to cross between parts.
Inputs may be any that keep to these rules, and one draw needn't show every extreme that they name: `decay_rate`: positive decay rate of each head.
All inputs are finite; a program needn't handle non-finite values.
Results may differ from a plain program's by a relative error of at most 0.014.
Values may be sent and summed in bfloat16 or wider, within the bound.
A program may use at most 128 MiB of HBM per device.

v0:
```python
import jax
import jax.numpy as jnp
from jax import lax
from jax.sharding import PartitionSpec as P

SPAN = 256
CH = 4096


def from_behind(block, axis, distance):
    devices = range(lax.axis_size(axis))
    route = [(i - distance, i) for i in devices if i - distance in devices]
    return lax.ppermute(block, axis, route)


def carried_in(value, axis, combine, identity):
    size, position = (lax.axis_size(axis), lax.axis_index(axis))
    everything = jax.tree.map(lambda part: lax.all_gather(part, axis), value)
    start = jax.tree.map(
        lambda part, zero: jnp.broadcast_to(jnp.asarray(zero, part.dtype), part.shape),
        value,
        identity,
    )

    def hop(k, before):
        reached = k < position
        new = combine(before, jax.tree.map(lambda part: part[k], everything))
        return jax.tree.map(lambda a, b: jnp.where(reached, a, b), new, before)

    return lax.fori_loop(0, size, hop, start)


def conv_silu(signal, before, weights):
    length = signal.shape[0]
    tap_count = weights.shape[0]
    joined = jnp.concatenate([before, signal], axis=0).astype(jnp.float32)
    summed = weights[tap_count - 1] * joined[tap_count - 1 :]
    for tap_index in range(tap_count - 1):
        summed = summed + weights[tap_index] * joined[tap_index : tap_index + length]
    return jax.nn.silu(summed).astype(jnp.bfloat16)


def link_states(earlier, later):
    return (earlier[0] * later[0], later[0][:, None, None] * earlier[1] + later[1])


def local(
    x_in, b_in, c_in, z_in, dt_raw, decay_rate, d_skip, conv_x, conv_b, conv_c, norm_gain, w_out
):
    tok_count = x_in.shape[0]
    head_count = dt_raw.shape[1]
    x_width = x_in.shape[1]
    head_size = x_width // head_count
    state_width = b_in.shape[1]
    tap_count = conv_x.shape[0]
    span_count = tok_count // SPAN
    state_parts = lax.axis_size("state")
    state_index = lax.axis_index("state")
    own_heads = head_count // state_parts
    own_start = state_index * own_heads
    rim_start = tok_count - (tap_count - 1)
    packed = jnp.concatenate([x_in[rim_start:], b_in[rim_start:], c_in[rim_start:]], axis=1)
    arrived = from_behind(packed, "ctx", 1)
    x_conv = conv_silu(x_in, arrived[:, :x_width], conv_x)
    b_conv = conv_silu(b_in, arrived[:, x_width : x_width + state_width], conv_b)
    c_conv = conv_silu(c_in, arrived[:, x_width + state_width :], conv_c)
    step_size = jax.nn.softplus(dt_raw).reshape(span_count, SPAN, head_count)
    cumulative = jnp.cumsum(-decay_rate * step_size, axis=1)
    span_total = cumulative[:, -1, :]
    b_blocks = b_conv.reshape(span_count, SPAN, state_width)
    c_blocks = c_conv.reshape(span_count, SPAN, state_width)
    x_heads = x_conv.reshape(span_count, SPAN, head_count, head_size).astype(jnp.float32)
    partial_inner = jnp.einsum(
        "ktn,ksn->kts", c_blocks, b_blocks, preferred_element_type=jnp.float32
    )
    inner_all = lax.psum(partial_inner.astype(jnp.bfloat16), "state").astype(jnp.float32)
    weighted = (
        (jnp.exp(span_total[:, None, :] - cumulative) * step_size)[..., None] * x_heads
    ).astype(jnp.bfloat16)
    span_states = jnp.einsum(
        "kthp,ktn->khpn", weighted, b_blocks, preferred_element_type=jnp.float32
    )
    running = jnp.zeros((head_count, head_size, state_width), jnp.float32)
    entering = []
    for span_id in range(span_count):
        entering.append(running)
        running = jnp.exp(span_total[span_id])[:, None, None] * running + span_states[span_id]
    block_decay = jnp.exp(jnp.sum(span_total, axis=0))
    prior = carried_in(
        (block_decay, running),
        "ctx",
        link_states,
        (jnp.ones_like(block_decay), jnp.zeros_like(running)),
    )
    before_span = jnp.exp(jnp.cumsum(span_total, axis=0) - span_total)
    states_in = (before_span[:, :, None, None] * prior[1] + jnp.stack(entering)).astype(
        jnp.bfloat16
    )
    cum_own = lax.dynamic_slice_in_dim(cumulative, own_start, own_heads, 2)
    inter_part = jnp.einsum(
        "ktn,khpn->kthp", c_blocks, states_in, preferred_element_type=jnp.float32
    )
    inter_part = inter_part * jnp.exp(cumulative)[..., None]
    inter_own = lax.psum_scatter(
        inter_part.reshape(tok_count, x_width), "state", scatter_dimension=1, tiled=True
    )
    x_own = lax.dynamic_slice_in_dim(x_heads, own_start, own_heads, 2)
    step_own = lax.dynamic_slice_in_dim(step_size, own_start, own_heads, 2)
    inputs_own = (step_own[..., None] * x_own).astype(jnp.bfloat16)
    cum_heads = jnp.transpose(cum_own, (0, 2, 1))
    log_gap = cum_heads[:, :, :, None] - cum_heads[:, :, None, :]
    causal = jnp.arange(SPAN)[:, None] >= jnp.arange(SPAN)[None, :]
    scores = (inner_all[:, None] * jnp.exp(jnp.where(causal, log_gap, -jnp.inf))).astype(
        jnp.bfloat16
    )
    intra_own = jnp.einsum(
        "khts,kshp->kthp", scores, inputs_own, preferred_element_type=jnp.float32
    )
    skip_own = lax.dynamic_slice_in_dim(d_skip, own_start, own_heads, 0)
    mixed = (intra_own + skip_own[:, None] * x_own).reshape(
        tok_count, own_heads * head_size
    ) + inter_own
    gated = mixed * jax.nn.silu(z_in.astype(jnp.float32))
    square_sum = lax.psum(jnp.sum(gated * gated, axis=1), ("state", "head"))
    mean_square = square_sum / CH
    normed = (gated * lax.rsqrt(mean_square + 1e-05)[:, None] * norm_gain).astype(jnp.bfloat16)
    weights_all = lax.all_gather(w_out, "ctx", axis=0, tiled=True)
    out_width = w_out.shape[1]
    block_width = normed.shape[1]
    head_parts = lax.axis_size("head")
    reordered = weights_all.reshape(head_parts, state_parts, block_width, out_width)
    reordered = jnp.transpose(reordered, (1, 0, 2, 3)).reshape(-1, out_width)
    result = jnp.dot(
        lax.all_gather(normed, ("state", "head"), axis=1, tiled=True),
        reordered,
        preferred_element_type=jnp.float32,
    )
    return result.astype(jnp.bfloat16)


def solution(mesh):
    return jax.shard_map(
        local,
        mesh=mesh,
        in_specs=(
            P(("groups", "ctx"), "head"),
            P(("groups", "ctx"), "state"),
            P(("groups", "ctx"), "state"),
            P(("groups", "ctx"), ("head", "state")),
            P(("groups", "ctx"), "head"),
            P("head"),
            P("head"),
            P(None, "head"),
            P(None, "state"),
            P(None, "state"),
            P(("head", "state")),
            P("ctx", ("state", "head")),
        ),
        out_specs=P(("groups", "ctx"), ("state", "head")),
        check_vma=False,
    )
```

profile of v0, /device:TPU:26, one launch (start us, length us, event | category | flops | bytes accessed | tf_op | source)
XLA Modules:
  0.0 571.1 jit_solution(9875607563149027762)
XLA Ops:
  9.6 1.3 collective-permute-start
  13.6 1.2 reduce-window.6
  16.6 2.2 maximum_convert_fusion
  18.8 3.8 fusion.19
  22.6 5.3 copy.59
  28.0 6.0 %reshape.94 = f32[2,256,32,64]{1,0,3,2:T(2,128)} reshape(f32[512,2048]{0,1:T(8,128)} %copy.59) | data formatting | bytes 8388608 | tf_op jit(solution)/shard_map/convert_element_type | solution.py:72
  34.3 4.2 multiply_convert_fusion.2
  39.1 1.3 fusion.17
  40.4 4.6 slice_add_fusion
  47.1 9.2 %all-reduce.1 = f32[128]{0:T(128)S(1)} all-reduce(f32[128]{0:T(128)S(1)} %exponential_dynamic-update-slice_fusion), channel_id=2, replica_groups=mesh['groups'=2,'ctx'=4,'state'=2,'head'=2] {'ctx'}, use_global_device_ids=true, to_apply=%add.1 | all-reduce | flops 128 | bytes 1024
  57.0 1.0 convolution_convert_fusion.1
  58.3 273.0 %all-gather.5.cloned.1.call-done = f32[4,32,64,512]{3,2,1,0:T(8,128)} async-done(((f32[1,32,64,512]{3,2,1,0:T(8,128)}), f32[4,32,64,512]{3,2,1,0:T(8,128)}) %all-gather.5.cloned.1.call-update) | async-done | bytes 16777232 | tf_op jit(solution)/shard_map/all_gather | solution.py:18
  331.3 26.0 %while.14 = (s32[]{:T(128)}, f32[32,64,512]{2,1,0:T(8,128)}, s32[]{:T(128)}, f32[4,32]{1,0:T(4,128)S(1)}, f32[4,32,64,512]{3,2,1,0:T(8,128)}, /*index=5*/s32[]{:T(128)}, s32[]{:T(128)}) while((s32[]{:T(128)}, f32[32,64,512]{2,1,0:T(8,128)}, s32[]{:T(128)}, f32[4,32]{1,0:T(4,128)S(1)}, f32[4,32,64,512]{3,2,1,0:T(8,128)}, ...), condition=%wide.region_6.7_spmd.clone, body=%wide.region_5.6_spmd.clone.sunk | while | flops 4194308 | bytes 12583409 | solution.py:30
  331.3 5.5 fusion.45
  336.9 6.8 %fusion.45 = f32[32,64,512]{2,1,0:T(8,128)} fusion(f32[4,32,64,512]{3,2,1,0:T(8,128)} %get-tuple-element.205, s32[]{:T(128)S(6)} %copy.97, f32[32,64,512]{2,1,0:T(8,128)} %get-tuple-element.195, f32[32]{0:T(128)S(1)} %dynamic-slice_bitcast_fusion.2, pred[]{:T(512)S(6)} %compare.4, pred[]{:T(512)S(6)} %lt.29), kind=kLoop, calls=%fused_computation.1.clone.1 | loop fusion | flops 4194304 | bytes 12583046 | tf_op jit(solution)/shard_map/while/body/eval_jaxpr/jit(_where)/select_n | solution.py:28
  343.7 6.8 %fusion.45 = f32[32,64,512]{2,1,0:T(8,128)} fusion(f32[4,32,64,512]{3,2,1,0:T(8,128)} %get-tuple-element.205, s32[]{:T(128)S(6)} %copy.97, f32[32,64,512]{2,1,0:T(8,128)} %get-tuple-element.195, f32[32]{0:T(128)S(1)} %dynamic-slice_bitcast_fusion.2, pred[]{:T(512)S(6)} %compare.4, pred[]{:T(512)S(6)} %lt.29), kind=kLoop, calls=%fused_computation.1.clone.1 | loop fusion | flops 4194304 | bytes 12583046 | tf_op jit(solution)/shard_map/while/body/eval_jaxpr/jit(_where)/select_n | solution.py:28
  350.5 6.8 %fusion.45 = f32[32,64,512]{2,1,0:T(8,128)} fusion(f32[4,32,64,512]{3,2,1,0:T(8,128)} %get-tuple-element.205, s32[]{:T(128)S(6)} %copy.97, f32[32,64,512]{2,1,0:T(8,128)} %get-tuple-element.195, f32[32]{0:T(128)S(1)} %dynamic-slice_bitcast_fusion.2, pred[]{:T(512)S(6)} %compare.4, pred[]{:T(512)S(6)} %lt.29), kind=kLoop, calls=%fused_computation.1.clone.1 | loop fusion | flops 4194304 | bytes 12583046 | tf_op jit(solution)/shard_map/while/body/eval_jaxpr/jit(_where)/select_n | solution.py:28
  357.3 4.2 broadcast_multiply_fusion
  361.6 3.4 copy.68
  364.9 2.4 copy.79
  369.3 2.3 constant_dynamic-slice_fusion.1
  371.6 1.0 convert_element_type.61
  372.6 2.3 bitcast_add_fusion.1
  374.9 1.6 copy.64
  376.7 45.1 %reduce-scatter.2.cloned.1.call-done = f32[512,1024]{0,1:T(8,128)} async-done(((f32[512,2048]{0,1:T(8,128)}), f32[512,1024]{0,1:T(8,128)}) %reduce-scatter.2.cloned.1.call-update) | async-done | bytes 2097168 | tf_op jit(solution)/shard_map/reduce_scatter | solution.py:104
  421.8 3.7 multiply_reduce_fusion
  425.5 6.9 %psum.15 = f32[512]{0:T(512)S(1)} all-reduce(f32[512]{0:T(512)S(1)} %get-tuple-element.132), channel_id=1, replica_groups=mesh['groups'=2,'ctx'=4,'state'=2,'head'=2] {'state','head'}, use_global_device_ids=true, to_apply=%region_9.10 | all-reduce | flops 512 | bytes 4096 | tf_op jit(solution)/shard_map/psum | solution.py:124
  432.4 2.8 multiply_convert_fusion.4
  435.3 82.4 %all-gather.9.cloned.1.call-done = bf16[4096,1024]{1,0:T(8,128)(2,1)} async-done(((bf16[1024,1024]{1,0:T(8,128)(2,1)}), bf16[4096,1024]{1,0:T(8,128)(2,1)}) %all-gather.9.cloned.1.call-update) | async-done | bytes 8388624 | tf_op jit(solution)/shard_map/all_gather | solution.py:127
  517.7 7.6 %copy.70 = bf16[2,2,1024,1024]{3,2,1,0:T(8,128)(2,1)} copy(bf16[2,2,1024,1024]{3,2,0,1:T(8,128)(2,1)} %bitcast.84) | data formatting | bytes 16777216 | tf_op jit(solution)/shard_map/transpose | solution.py:132
  525.3 28.6 %all-gather.7.cloned.1.call-done = bf16[512,4096]{0,1:T(8,128)(2,1)} async-done(((bf16[512,1024]{0,1:T(8,128)(2,1)}), bf16[512,4096]{0,1:T(8,128)(2,1)}) %all-gather.7.cloned.1.call-update) | async-done | bytes 4194320 | tf_op jit(solution)/shard_map/all_gather | solution.py:134
  553.9 10.1 %convolution_convert_fusion = bf16[512,1024]{1,0:T(8,128)(2,1)} fusion(bf16[512,4096]{0,1:T(8,128)(2,1)} %all-gather.7.cloned.1.call-done, bf16[4096,1024]{1,0:T(8,128)(2,1)} %bitcast.85), kind=kOutput, calls=%fused_computation.40 | convolution fusion | flops 4295491584 | bytes 13631488 | tf_op jit(solution)/shard_map/dot_general | solution.py:133
  (71 shorter events, 12.0 us)
Async XLA Ops:
  7.4 323.9 %all-gather.5.cloned.1.call-start = ((), (), s32[]{:S(2)}) async-start(), calls=%async_computation.2 | async-start | bytes 20971520 | tf_op jit(solution)/shard_map/all_gather | solution.py:18
  9.6 7.0 %collective-permute-start = (bf16[3,3072]{1,0:T(4,128)(2,1)S(1)}, bf16[3,3072]{1,0:T(4,128)(2,1)S(1)}, u32[]{:S(2)}, u32[]{:S(2)}) collective-permute-start(bf16[3,3072]{1,0:T(4,128)(2,1)S(1)} %pad_maximum_fusion), channel_id=1, source_target_pairs={{0,4},{4,8},{8,12},{1,5},{5,9},{9,13},{2,6},{6,10},{10,14},{3,7},{... | collective-permute-start | bytes 55304 | tf_op jit(solution)/shard_map/ppermute | solution.py:13
  28.0 6.0 %copy-start.1 = (bf16[512,512]{1,0:T(8,128)(2,1)S(1)}, bf16[512,512]{1,0:T(8,128)(2,1)}, u32[]{:S(2)}) copy-start(bf16[512,512]{1,0:T(8,128)(2,1)} %param.16) | copy-start | bytes 1572868
  28.0 6.0 %copy-start.2 = (bf16[512,512]{1,0:T(8,128)(2,1)S(1)}, bf16[512,512]{1,0:T(8,128)(2,1)}, u32[]{:S(2)}) copy-start(bf16[512,512]{1,0:T(8,128)(2,1)} %param.15) | copy-start | bytes 1572868
  45.0 0.7 copy-start.6
  45.1 11.3 %copy-start.3 = (f32[4,512]{1,0:T(4,128)S(1)}, f32[4,512]{1,0:T(4,128)}, u32[]{:S(2)}) copy-start(f32[4,512]{1,0:T(4,128)} %param.23) | copy-start | bytes 24580
  45.1 326.5 %all-reduce.4.cloned.1.call-start = ((), (), s32[]{:S(2)}) async-start(), calls=%async_computation.1 | async-start | bytes 524288 | tf_op jit(solution)/shard_map/psum | solution.py:76
  58.1 363.8 %reduce-scatter.2.cloned.1.call-start = ((), (), s32[]{:S(2)}) async-start(), calls=%async_computation.3 | async-start | bytes 6291456 | tf_op jit(solution)/shard_map/reduce_scatter | solution.py:104
  367.4 1.2 copy-start
  367.4 1.8 copy-start.5
  367.4 150.3 %all-gather.9.cloned.1.call-start = ((), (), s32[]{:S(2)}) async-start(), calls=%async_computation.5 | async-start | bytes 10485760 | tf_op jit(solution)/shard_map/all_gather | solution.py:127
  368.1 185.8 %all-gather.7.cloned.1.call-start = ((), (), s32[]{:S(2)}) async-start(), calls=%async_computation.4 | async-start | bytes 5242880 | tf_op jit(solution)/shard_map/all_gather | solution.py:134
  376.7 55.7 %copy-start.4 = (f32[1024]{0:T(1024)S(1)}, f32[1024]{0:T(1024)}, u32[]{:S(2)}) copy-start(f32[1024]{0:T(1024)} %param.24) | copy-start | bytes 12292
Sparse Core Ops, SparseCore 0:
  45.2 286.0 all-gather.4
  369.8 147.8 all-gather.8
  519.3 34.5 all-gather.6
Sparse Core Ops, SparseCore 1:
  58.1 22.9 all-reduce.3
  367.5 54.3 reduce-scatter.1
where the time goes:
time: 575 us; the launch traced here: 571 us
  waiting for transfers between devices  430 us (75%)
  other arithmetic  53.5 us (9%)
  local copies, waits for them, and re-layouts  35.5 us (6%)
  matrix products  18.9 us (3%)
  blocking collectives  16.1 us (3%)
  between operations  15.5 us (3%)
    all_gather x1, waiting for transfers between devices, carried_in(): everything = jax.tree.map(lambda part: lax.all_gather(part, axis), value)  273 us
    all_gather x1, waiting for transfers between devices, local(): weights_all = lax.all_gather(w_out, 'ctx', axis=0, tiled=True)  82.4 us
    reduce_scatter x1, waiting for transfers between devices, local(): lax.psum_scatter(inter_part.reshape(tok_count, x_width), 'state', scatter...  45.1 us
    all_gather x1, waiting for transfers between devices, local(): lax.all_gather(normed, ('state', 'head'), axis=1, tiled=True)  28.6 us
    select_n x4, other arithmetic, hop(): return jax.tree.map(lambda a, b: jnp.where(reached, a, b), new, before)  26 us
  transfers between devices with their start and end apart: 6, of which 4 were waited for; matrix products, arithmetic and copies ran while one was open for 12% of the time, Pallas kernels for 0%

commit v1 on v0

v1 whole, which is shorter than its diff:
```python
import jax
import jax.numpy as jnp
from jax import lax
from jax.sharding import PartitionSpec as P

SPAN = 256
CHUNKS = 4


def conv_silu(signal, before, weights):
    length = signal.shape[0]
    taps = weights.shape[0]
    joined = jnp.concatenate([before, signal], axis=0).astype(jnp.float32)
    summed = weights[taps - 1] * joined[taps - 1 :]
    for k in range(taps - 1):
        summed = summed + weights[k] * joined[k : k + length]
    return jax.nn.silu(summed).astype(jnp.bfloat16)


def local(
    x_in, b_in, c_in, z_in, dt_raw, decay_rate, d_skip, conv_x, conv_b, conv_c, norm_gain, w_out
):
    f32, bf16 = jnp.float32, jnp.bfloat16
    parts = lax.axis_size("state")
    part = lax.axis_index("state")
    ctx = lax.axis_size("ctx")
    me = lax.axis_index("ctx")
    groups = lax.axis_size("groups")
    tokens = x_in.shape[0]
    heads = dt_raw.shape[1] // parts
    width = x_in.shape[1] // parts
    size = width // heads
    nb = b_in.shape[1]
    taps = conv_x.shape[0]
    spans = tokens // SPAN
    total_channels = width * parts * lax.axis_size("head")

    rows = w_out.shape[0] // groups
    w_half = lax.dynamic_slice_in_dim(w_out, lax.axis_index("groups") * rows, rows, 0)
    w_all = lax.all_gather(w_half, ("ctx", "groups"), axis=0, tiled=True)

    own = lambda a, axis: lax.dynamic_slice_in_dim(
        a, part * (a.shape[axis] // parts), a.shape[axis] // parts, axis
    )
    x_own, dt_own, rate, skip, taps_x = (
        own(x_in, 1), own(dt_raw, 1), own(decay_rate, 0), own(d_skip, 0), own(conv_x, 1)
    )
    rim = tokens - (taps - 1)
    packed = jnp.concatenate([x_own[rim:], b_in[rim:], c_in[rim:]], axis=1)
    onward = [(i, i + 1) for i in range(ctx - 1)]
    arrived = lax.ppermute(packed, "ctx", onward)
    bc = conv_silu(
        jnp.concatenate([b_in, c_in], axis=1),
        arrived[:, width:],
        jnp.concatenate([conv_b, conv_c], axis=1),
    )
    bc_all = lax.all_gather(bc, "state", axis=0)
    x_conv = conv_silu(x_own, arrived[:, :width], taps_x)
    b = jnp.concatenate([bc_all[i, :, :nb] for i in range(parts)], axis=1)
    c = jnp.concatenate([bc_all[i, :, nb:] for i in range(parts)], axis=1)
    b = b.reshape(spans, SPAN, parts * nb)
    c = c.reshape(spans, SPAN, parts * nb)
    step = jax.nn.softplus(dt_own).reshape(spans, SPAN, heads)
    causal = jnp.arange(SPAN)[:, None] >= jnp.arange(SPAN)[None, :]
    cum = jnp.einsum(
        "ts,ksh->kth", causal.astype(f32), -rate * step, precision=lax.Precision.HIGHEST
    )
    last = cum[:, -1, :]
    x_heads = x_conv.reshape(spans, SPAN, heads, size).astype(f32)
    weighted = ((jnp.exp(last[:, None, :] - cum) * step)[..., None] * x_heads).astype(bf16)
    update = jnp.einsum("kthp,ktn->khpn", weighted, b, preferred_element_type=f32)
    running = jnp.zeros_like(update[0])
    entering, reach, gain = [], [], jnp.ones_like(last[0])
    for k in range(spans):
        entering.append(running)
        reach.append(gain)
        decay = jnp.exp(last[k])
        running = decay[:, None, None] * running + update[k]
        gain = gain * decay
    some = heads // CHUNKS
    final = running.reshape(CHUNKS, some, size, -1)
    gain_c = gain.reshape(CHUNKS, some)
    prior = jnp.zeros(final.shape, bf16)
    got = jnp.zeros(final.shape[1:], bf16)
    for t in range(CHUNKS + ctx - 1):
        place = jnp.clip(t - me, 0, CHUNKS - 1)
        fits = (t >= me) & (t - me < CHUNKS)
        if t > 0:
            old = lax.dynamic_index_in_dim(prior, place, 0, keepdims=False)
            prior = lax.dynamic_update_index_in_dim(prior, jnp.where(fits, got, old), place, 0)
        if t < CHUNKS + ctx - 2:
            mine = lax.dynamic_index_in_dim(final, place, 0, keepdims=False)
            factor = lax.dynamic_index_in_dim(gain_c, place, 0, keepdims=False)
            send = (factor[:, None, None] * got.astype(f32) + mine).astype(bf16)
            got = lax.ppermute(send, "ctx", onward)
    prior = prior.reshape(running.shape).astype(f32)

    inner = jnp.einsum("ktn,ksn->kts", c, b, preferred_element_type=f32)
    cum_heads = jnp.transpose(cum, (0, 2, 1))
    gap = cum_heads[:, :, :, None] - cum_heads[:, :, None, :]
    scores = (inner[:, None] * jnp.exp(jnp.where(causal, gap, -jnp.inf))).astype(bf16)
    inputs = (step[..., None] * x_heads).astype(bf16)
    intra = jnp.einsum("khts,kshp->kthp", scores, inputs, preferred_element_type=f32)
    states = (jnp.stack(reach)[:, :, None, None] * prior + jnp.stack(entering)).astype(bf16)
    inter = jnp.einsum("ktn,khpn->kthp", c, states, preferred_element_type=f32)
    mixed = intra + skip[:, None] * x_heads + jnp.exp(cum)[..., None] * inter
    gated = mixed.reshape(tokens, width) * jax.nn.silu(z_in.astype(f32))
    square = lax.psum(jnp.sum(gated * gated, axis=1), ("state", "head"))
    everything = lax.all_gather(
        (gated * norm_gain).astype(bf16), ("head", "state"), axis=1, tiled=True
    )
    result = jnp.dot(everything, w_all, preferred_element_type=f32)
    result = result * lax.rsqrt(square / total_channels + 1e-05)[:, None]
    return result.astype(bf16)


def solution(mesh):
    return jax.shard_map(
        local,
        mesh=mesh,
        in_specs=(
            P(("groups", "ctx"), "head"),
            P(("groups", "ctx"), "state"),
            P(("groups", "ctx"), "state"),
            P(("groups", "ctx"), ("head", "state")),
            P(("groups", "ctx"), "head"),
            P("head"),
            P("head"),
            P(None, "head"),
            P(None, "state"),
            P(None, "state"),
            P(("head", "state")),
            P("ctx", ("state", "head")),
        ),
        out_specs=P(("groups", "ctx"), ("state", "head")),
        check_vma=False,
    )
```

time: 575 us -> 356 us (0.62)
  waiting for transfers between devices: 430 us -> 251 us
  other arithmetic: 53.5 us -> 29.3 us
  local copies, waits for them, and re-layouts: 35.5 us -> 24 us
  blocking collectives: 16.1 us -> 5.89 us
  starting transfers between devices: 1.64 us -> 9.3 us
    all_gather x3, waiting for transfers between devices: 384 us -> 175 us  [the longest x1 126 us: local(): w_all = lax.all_gather(w_half, ('ctx', 'groups'), axis=0, tiled=True)]
    ppermute x1 -> x7, waiting for transfers between devices: 0.01 us -> 76.5 us  [the longest x6 62.9 us: local(): got = lax.ppermute(send, 'ctx', onward)]
    reduce_scatter x1 -> x0, waiting for transfers between devices: 45.1 us -> none  [local(): lax.psum_scatter(inter_part.reshape(tok_count, x_width), 'state', scatter...]
    select_n x5 -> x1, other arithmetic: 26.8 us -> 0.03 us  [local(): step = jax.nn.softplus(dt_own).reshape(spans, SPAN, heads)]
    unnamed x1 -> x0, blocking collectives: 9.18 us -> none
    convert_element_type x2 -> x1, local copies, waits for them, and re-layouts: 11.3 us -> 2.56 us  [local(): x_heads = x_conv.reshape(spans, SPAN, heads, size).astype(f32)]
    ppermute x1 -> x7, starting transfers between devices: 1.29 us -> 9.21 us  [the longest x6 7.92 us: local(): got = lax.ppermute(send, 'ctx', onward)]
    transpose x2 -> x0, local copies, waits for them, and re-layouts: 7.57 us -> none  [the longest x1 7.57 us: local(): reordered = jnp.transpose(reordered, (1, 0, 2, 3)).reshape(-1, out_width)]
  transfers between devices with their start and end apart: 6 -> 10, of which waited for: 4 -> 10; matrix products, arithmetic and copies ran while one was open for 12% -> 6% of each run, Pallas kernels for 0% -> 0%
where the time goes in v1:
time: 356 us; the launch traced here: 351 us
  waiting for transfers between devices  251 us (71%)
  other arithmetic  29.3 us (8%)
  local copies, waits for them, and re-layouts  24 us (7%)
  matrix products  17.4 us (5%)
  between operations  13.8 us (4%)
  starting transfers between devices  9.3 us (3%)
  blocking collectives  5.89 us (2%)
    all_gather x1, waiting for transfers between devices, local(): w_all = lax.all_gather(w_half, ('ctx', 'groups'), axis=0, tiled=True)  126 us
    ppermute x6, waiting for transfers between devices, local(): got = lax.ppermute(send, 'ctx', onward)  62.9 us
    all_gather x1, waiting for transfers between devices, local(): lax.all_gather((gated * norm_gain).astype(bf16), ('head', 'state'), axis=...  26.4 us
    all_gather x1, waiting for transfers between devices, local(): bc_all = lax.all_gather(bc, 'state', axis=0)  22.5 us
    ppermute x1, waiting for transfers between devices, local(): arrived = lax.ppermute(packed, 'ctx', onward)  13.6 us
    dot_general x1, matrix products, local(): result = jnp.dot(everything, w_all, preferred_element_type=f32)  10.3 us
    ppermute x6, starting transfers between devices, local(): got = lax.ppermute(send, 'ctx', onward)  7.92 us
  transfers between devices with their start and end apart: 10, of which 10 were waited for; matrix products, arithmetic and copies ran while one was open for 6% of the time, Pallas kernels for 0%

profile of v1, /device:TPU:26, one launch (start us, length us, event | category | flops | bytes accessed | tf_op | source)
XLA Modules:
  0.0 351.2 jit_solution(670605275330133213)
XLA Ops:
  9.5 1.3 collective-permute-start
  11.5 13.6 %collective-permute-done = bf16[3,2048]{0,1:T(8,128)(2,1)} collective-permute-done((bf16[3,2048]{0,1:T(8,128)(2,1)S(1)}, bf16[3,2048]{0,1:T(8,128)(2,1)}, u32[]{:S(2)}, u32[]{:S(2)}) %collective-permute-start) | collective-permute-done | bytes 12320 | tf_op jit(solution)/shard_map/ppermute | solution.py:51
  26.8 3.3 multiply_convert_fusion.5
  31.9 3.5 fusion.31
  35.3 2.6 reshape.91
  37.9 3.1 multiply_convert_fusion.4
  41.0 22.5 %all-gather.9.cloned.1.call-done = bf16[1024,1024]{0,1:T(8,128)(2,1)} async-done(((bf16[512,1024]{0,1:T(8,128)(2,1)}), bf16[1024,1024]{0,1:T(8,128)(2,1)}) %all-gather.9.cloned.1.call-update) | async-done | bytes 2097168 | tf_op jit(solution)/shard_map/all_gather | solution.py:57
  63.4 3.9 %copy.66 = bf16[1024,1024]{1,0:T(8,128)(2,1)} copy(bf16[1024,1024]{0,1:T(8,128)(2,1)} %all-gather.9.cloned.1.call-done) | data formatting | bytes 4194304 | tf_op jit(solution)/shard_map/all_gather | solution.py:57
  67.4 2.7 fusion.51
  71.3 5.4 %fusion.50 = (f32[1,16,64,1024]{3,2,1,0:T(8,128)}, f32[1,16,64,1024]{3,2,1,0:T(8,128)}, f32[1,16,64,1024]{3,2,1,0:T(8,128)}) fusion(f32[2,16,64,1024]{3,2,1,0:T(8,128)S(1)} %fusion.20, f32[16]{0:T(128)S(1)} %get-tuple-element.7), kind=kLoop, calls=%fused_computation.124 | loop fusion | flops 1048576 | bytes 20971584 | tf_op jit(solution)/shard_map/slice | solution.py:78
  76.7 4.6 %multiply_add_fusion = f32[4,4,64,1024]{3,2,1,0:T(8,128)S(1)} fusion(f32[4,4,64,1024]{3,2,1,0:T(8,128)} %bitcast.122, f32[4,4,64,1024]{3,2,1,0:T(8,128)} %bitcast.121, f32[4,4]{1,0:T(4,128)S(1)} %get-tuple-element.38, f32[4,4]{1,0:T(4,128)S(1)} %exp.66), kind=kLoop, calls=%fused_computation.5 | loop fusion | flops 3145728 | bytes 12583040 | tf_op jit(solution)/shard_map/add | solution.py:78
  81.5 1.5 collective-permute-start.1
  82.9 14.1 %collective-permute-done.1 = bf16[4,64,1024]{2,1,0:T(8,128)(2,1)S(1)} collective-permute-done((bf16[4,64,1024]{2,1,0:T(8,128)(2,1)S(1)}, bf16[4,64,1024]{2,1,0:T(8,128)(2,1)S(1)}, u32[]{:S(2)}, u32[]{:S(2)}) %collective-permute-start.1) | collective-permute-done | bytes 524320 | tf_op jit(solution)/shard_map/ppermute | solution.py:95
  97.2 1.3 collective-permute-start.2
  98.5 13.4 %collective-permute-done.2 = bf16[4,64,1024]{2,1,0:T(8,128)(2,1)S(1)} collective-permute-done((bf16[4,64,1024]{2,1,0:T(8,128)(2,1)S(1)}, bf16[4,64,1024]{2,1,0:T(8,128)(2,1)S(1)}, u32[]{:S(2)}, u32[]{:S(2)}) %collective-permute-start.2) | collective-permute-done | bytes 524320 | tf_op jit(solution)/shard_map/ppermute | solution.py:95
  115.2 1.5 copy.63
  116.8 2.1 fusion.32
  118.9 8.9 %collective-permute-done.3 = bf16[4,64,1024]{2,1,0:T(8,128)(2,1)} collective-permute-done((bf16[4,64,1024]{2,1,0:T(8,128)(2,1)}, bf16[4,64,1024]{2,1,0:T(8,128)(2,1)}, u32[]{:S(2)}, u32[]{:S(2)}) %collective-permute-start.3) | collective-permute-done | bytes 524320 | tf_op jit(solution)/shard_map/ppermute | solution.py:95
  129.1 1.3 collective-permute-start.4
  130.4 2.1 fusion
  133.7 8.2 %collective-permute-done.4 = bf16[4,64,1024]{2,1,0:T(8,128)(2,1)S(1)} collective-permute-done((bf16[4,64,1024]{2,1,0:T(8,128)(2,1)S(1)}, bf16[4,64,1024]{2,1,0:T(8,128)(2,1)S(1)}, u32[]{:S(2)}, u32[]{:S(2)}) %collective-permute-start.4) | collective-permute-done | bytes 524320 | tf_op jit(solution)/shard_map/ppermute | solution.py:95
  145.1 9.0 %collective-permute-done.5 = bf16[4,64,1024]{2,1,0:T(8,128)(2,1)S(1)} collective-permute-done((bf16[4,64,1024]{2,1,0:T(8,128)(2,1)S(1)}, bf16[4,64,1024]{2,1,0:T(8,128)(2,1)S(1)}, u32[]{:S(2)}, u32[]{:S(2)}) %collective-permute-start.5) | collective-permute-done | bytes 524320 | tf_op jit(solution)/shard_map/ppermute | solution.py:95
  156.2 9.3 %collective-permute-done.6 = bf16[4,64,1024]{2,1,0:T(8,128)(2,1)S(1)} collective-permute-done((bf16[4,64,1024]{2,1,0:T(8,128)(2,1)S(1)}, bf16[4,64,1024]{2,1,0:T(8,128)(2,1)S(1)}, u32[]{:S(2)}, u32[]{:S(2)}) %collective-permute-start.6) | collective-permute-done | bytes 524320 | tf_op jit(solution)/shard_map/ppermute | solution.py:95
  166.3 1.5 copy-done.4
  168.1 1.4 fusion.19
  169.5 1.6 copy.62
  171.9 1.8 multiply_reduce_fusion
  173.7 2.3 constant_dynamic-slice_fusion.1
  176.0 5.9 %psum.7 = f32[512]{0:T(512)S(1)} all-reduce(f32[512]{0:T(512)S(1)} %get-tuple-element.11), channel_id=1, replica_groups=mesh['groups'=2,'ctx'=4,'state'=2,'head'=2] {'state','head'}, use_global_device_ids=true, to_apply=%region_1.2 | all-reduce | flops 512 | bytes 4096 | tf_op jit(solution)/shard_map/psum | solution.py:108
  181.9 26.4 %all-gather.5.cloned.1.call-done = bf16[512,4096]{0,1:T(8,128)(2,1)} async-done(((bf16[512,1024]{0,1:T(8,128)(2,1)}), bf16[512,4096]{0,1:T(8,128)(2,1)}) %all-gather.5.cloned.1.call-update) | async-done | bytes 4194320 | tf_op jit(solution)/shard_map/all_gather | solution.py:109
  208.3 126.1 %all-gather.7.cloned.1.call-done = bf16[4096,1024]{1,0:T(8,128)(2,1)} async-done(((bf16[512,1024]{1,0:T(8,128)(2,1)}), bf16[4096,1024]{1,0:T(8,128)(2,1)}) %all-gather.7.cloned.1.call-update) | async-done | bytes 8388624 | tf_op jit(solution)/shard_map/all_gather | solution.py:40
  334.4 10.3 %multiply_convert_fusion.2 = bf16[512,1024]{1,0:T(8,128)(2,1)} fusion(bf16[512,4096]{0,1:T(8,128)(2,1)} %all-gather.5.cloned.1.call-done, bf16[4096,1024]{1,0:T(8,128)(2,1)} %all-gather.7.cloned.1.call-done, f32[512]{0:T(512)S(1)} %add_rsqrt_fusion), kind=kOutput, calls=%fused_computation.36 | convolution fusion | flops 4296015872 | bytes 13633536 | tf_op jit(solution)/shard_map/dot_general | solution.py:112
  (109 shorter events, 21.0 us)
Async XLA Ops:
  6.5 1.9 copy-start
  6.5 56.9 %all-gather.9.cloned.1.call-start = ((), (), s32[]{:S(2)}) async-start(), calls=%async_computation.2 | async-start | bytes 3145728 | tf_op jit(solution)/shard_map/all_gather | solution.py:57
  8.6 2.2 copy-start.16
  8.6 2.3 copy-start.21
  8.6 2.3 copy-start.18
  8.6 2.4 copy-start.19
  8.6 2.4 copy-start.14
  9.2 2.1 copy-start.15
  9.5 15.7 %collective-permute-start = (bf16[3,2048]{0,1:T(8,128)(2,1)S(1)}, bf16[3,2048]{0,1:T(8,128)(2,1)}, u32[]{:S(2)}, u32[]{:S(2)}) collective-permute-start(bf16[3,2048]{0,1:T(8,128)(2,1)S(1)} %pad_maximum_fusion.6), channel_id=1, source_target_pairs={{0,4},{4,8},{8,12},{1,5},{5,9},{9,13},{2,6},{6,10},{10,14},{3,7},{... | collective-permute-start | bytes 36872 | tf_op jit(solution)/shard_map/ppermute | solution.py:51
  26.7 4.4 %copy-start.17 = (f32[4,2048]{1,0:T(4,128)S(1)}, f32[4,2048]{1,0:T(4,128)}, u32[]{:S(2)}) copy-start(f32[4,2048]{1,0:T(4,128)} %param.19) | copy-start | bytes 98308
  30.1 178.1 %all-gather.5.cloned.1.call-start = ((), (), s32[]{:S(2)}) async-start(), calls=%async_computation | async-start | bytes 5242880 | tf_op jit(solution)/shard_map/all_gather | solution.py:109
  70.1 1.3 copy-start.11
  70.1 1.3 copy-start.12
  81.3 32.5 %copy-start.2 = (f32[4,4,64,1024]{3,2,1,0:T(8,128)}, f32[4,4,64,1024]{3,2,1,0:T(8,128)S(1)}, u32[]{:S(2)}) copy-start(f32[4,4,64,1024]{3,2,1,0:T(8,128)S(1)} %multiply_add_fusion) | copy-start | bytes 12582916
  81.5 15.6 %collective-permute-start.1 = (bf16[4,64,1024]{2,1,0:T(8,128)(2,1)S(1)}, bf16[4,64,1024]{2,1,0:T(8,128)(2,1)S(1)}, u32[]{:S(2)}, u32[]{:S(2)}) collective-permute-start(bf16[4,64,1024]{2,1,0:T(8,128)(2,1)S(1)} %fusion.28), channel_id=1, source_target_pairs={{0,4},{4,8},{8,12},{1,5},{5,9},{9,13},{2,6},{6,10},{10,14},{3,7},{... | collective-permute-start | bytes 1572872 | tf_op jit(solution)/shard_map/ppermute | solution.py:95
  97.0 16.8 %copy-start.7 = (bf16[4,64,1024]{2,1,0:T(8,128)(2,1)}, bf16[4,64,1024]{2,1,0:T(8,128)(2,1)S(1)}, u32[]{:S(2)}) copy-start(bf16[4,64,1024]{2,1,0:T(8,128)(2,1)S(1)} %collective-permute-done.1) | copy-start | bytes 1572868
  97.0 18.1 %copy-start.22 = (f32[32]{0:T(128)S(1)}, f32[32]{0:T(128)}, u32[]{:S(2)}) copy-start(f32[32]{0:T(128)} %param.18) | copy-start | bytes 388
  97.2 14.7 %collective-permute-start.2 = (bf16[4,64,1024]{2,1,0:T(8,128)(2,1)S(1)}, bf16[4,64,1024]{2,1,0:T(8,128)(2,1)S(1)}, u32[]{:S(2)}, u32[]{:S(2)}) collective-permute-start(bf16[4,64,1024]{2,1,0:T(8,128)(2,1)S(1)} %fusion.27), channel_id=1, source_target_pairs={{0,4},{4,8},{8,12},{1,5},{5,9},{9,13},{2,6},{6,10},{10,14},{3,7},{... | collective-permute-start | bytes 1572872 | tf_op jit(solution)/shard_map/ppermute | solution.py:95
  111.9 0.8 copy-start.9
  113.8 14.1 %collective-permute-start.3 = (bf16[4,64,1024]{2,1,0:T(8,128)(2,1)}, bf16[4,64,1024]{2,1,0:T(8,128)(2,1)}, u32[]{:S(2)}, u32[]{:S(2)}) collective-permute-start(bf16[4,64,1024]{2,1,0:T(8,128)(2,1)} %fusion.26), channel_id=1, source_target_pairs={{0,4},{4,8},{8,12},{1,5},{5,9},{9,13},{2,6},{6,10},{10,14},{3,7},{... | collective-permute-start | bytes 1572872 | tf_op jit(solution)/shard_map/ppermute | solution.py:95
  116.8 11.1 %copy-start.3 = (f32[4,4,64,1024]{3,2,1,0:T(8,128)S(1)}, f32[4,4,64,1024]{3,2,1,0:T(8,128)}, u32[]{:S(2)}) copy-start(f32[4,4,64,1024]{3,2,1,0:T(8,128)} %copy-done.2) | copy-start | bytes 12582916
  118.9 11.5 %copy-start.13 = (bf16[2,256,16,64]{1,0,3,2:T(2,128)(2,1)S(1)}, bf16[2,256,16,64]{1,0,3,2:T(2,128)(2,1)}, u32[]{:S(2)}) copy-start(bf16[2,256,16,64]{1,0,3,2:T(2,128)(2,1)} %get-tuple-element.14) | copy-start | bytes 3145732
  129.1 12.8 %collective-permute-start.4 = (bf16[4,64,1024]{2,1,0:T(8,128)(2,1)S(1)}, bf16[4,64,1024]{2,1,0:T(8,128)(2,1)S(1)}, u32[]{:S(2)}, u32[]{:S(2)}) collective-permute-start(bf16[4,64,1024]{2,1,0:T(8,128)(2,1)S(1)} %fusion.25), channel_id=1, source_target_pairs={{0,4},{4,8},{8,12},{1,5},{5,9},{9,13},{2,6},{6,10},{10,14},{3,7},{... | collective-permute-start | bytes 1572872 | tf_op jit(solution)/shard_map/ppermute | solution.py:95
  132.5 1.0 copy-start.8
  133.6 9.9 %copy-start.10 = (bf16[4,64,1024]{2,1,0:T(8,128)(2,1)S(1)}, bf16[4,64,1024]{2,1,0:T(8,128)(2,1)}, u32[]{:S(2)}) copy-start(bf16[4,64,1024]{2,1,0:T(8,128)(2,1)} %copy-done.9) | copy-start | bytes 1572868
  142.2 11.9 %collective-permute-start.5 = (bf16[4,64,1024]{2,1,0:T(8,128)(2,1)S(1)}, bf16[4,64,1024]{2,1,0:T(8,128)(2,1)S(1)}, u32[]{:S(2)}, u32[]{:S(2)}) collective-permute-start(bf16[4,64,1024]{2,1,0:T(8,128)(2,1)S(1)} %fusion.24), channel_id=1, source_target_pairs={{0,4},{4,8},{8,12},{1,5},{5,9},{9,13},{2,6},{6,10},{10,14},{3,7},{... | collective-permute-start | bytes 1572872 | tf_op jit(solution)/shard_map/ppermute | solution.py:95
  154.3 11.1 %collective-permute-start.6 = (bf16[4,64,1024]{2,1,0:T(8,128)(2,1)S(1)}, bf16[4,64,1024]{2,1,0:T(8,128)(2,1)S(1)}, u32[]{:S(2)}, u32[]{:S(2)}) collective-permute-start(bf16[4,64,1024]{2,1,0:T(8,128)(2,1)S(1)} %fusion.23), channel_id=1, source_target_pairs={{0,4},{4,8},{8,12},{1,5},{5,9},{9,13},{2,6},{6,10},{10,14},{3,7},{... | collective-permute-start | bytes 1572872 | tf_op jit(solution)/shard_map/ppermute | solution.py:95
  165.6 2.2 copy-start.4
  165.6 2.3 copy-start.5
  165.6 2.4 copy-start.6
  173.6 160.7 %all-gather.7.cloned.1.call-start = ((), (), s32[]{:S(2)}) async-start(), calls=%async_computation.1 | async-start | bytes 9437184 | tf_op jit(solution)/shard_map/all_gather | solution.py:40
  334.4 10.3 %copy-start.1 = (bf16[512,2048]{1,0:T(8,128)(2,1)S(1)}, bf16[512,2048]{1,0:T(8,128)(2,1)}, u32[]{:S(2)}) copy-start(bf16[512,2048]{1,0:T(8,128)(2,1)} %param.12) | copy-start | bytes 6291460
  (1 other events, 0.7 us)
Sparse Core Ops, SparseCore 0:
  30.3 33.1 all-gather.8
  173.8 34.4 all-gather.4
  210.4 123.9 all-gather.6

commit v2 on v1

v2 whole, which is shorter than its diff:
```python
import functools

import jax
import jax.numpy as jnp
from jax import lax
from jax.experimental import pallas as pl
from jax.experimental.pallas import tpu as pltpu
from jax.sharding import PartitionSpec as P

SPAN = 256
CHUNK = 256


def conv_silu(signal, before, weights):
    length = signal.shape[0]
    taps = weights.shape[0]
    joined = jnp.concatenate([before, signal], axis=0).astype(jnp.float32)
    summed = weights[taps - 1] * joined[taps - 1 :]
    for k in range(taps - 1):
        summed = summed + weights[k] * joined[k : k + length]
    return jax.nn.silu(summed).astype(jnp.bfloat16)


def kernel(
    axes, w_ref, final_ref, factor_ref, reach_ref, entering_ref, c_ref, base_ref, grow_ref, z_ref,
    gain_ref, o_ref, w_all, prior, outgoing, gates, squares, total,
    wr_send, wr_recv, wl_send, wl_recv, wy_send, wy_recv, st_send, st_recv,
    gx_send, gx_recv, gc_send, gc_recv, sq_send, sq_recv,
):
    f32, bf16 = jnp.float32, jnp.bfloat16
    G, C, S, H = axes
    g, me, s, h = (lax.axis_index(a) for a in ("groups", "ctx", "state", "head"))
    rows = w_ref.shape[0]
    part = rows // G
    K, nstate, cw = prior.shape
    tokens = c_ref.shape[0]
    spans = tokens // SPAN
    remote = functools.partial(
        pltpu.make_async_remote_copy, device_id_type=pl.DeviceIdType.MESH
    )

    others = [(a, b) for a in range(H) for b in range(S) if a or b]
    barrier = pltpu.get_barrier_semaphore()

    def greet(to):
        pl.semaphore_signal(barrier, inc=1, device_id=to, device_id_type=pl.DeviceIdType.MESH)

    pl.when(me > 0)(lambda: greet({"ctx": me - 1}))
    pl.when(me < C - 1)(lambda: greet({"ctx": me + 1}))
    for a in range(1, G):
        greet({"groups": lax.rem(g + a, G)})
    for a, b in others:
        greet({"head": lax.rem(h + a, H), "state": lax.rem(s + b, S)})
    peers = G - 1 + len(others) + (me > 0).astype(jnp.int32) + (me < C - 1).astype(jnp.int32)
    pl.semaphore_wait(barrier, peers)

    def piece(j, half):
        return w_all.at[pl.ds(pl.multiple_of(j * rows + half * part, part), part)]

    def right(k, j):
        return remote(piece(j, g), piece(j, g), wr_send.at[k], wr_recv.at[k], device_id={"ctx": me + 1})

    def left(k, j):
        return remote(piece(j, g), piece(j, g), wl_send.at[k], wl_recv.at[k], device_id={"ctx": me - 1})

    def across(way, k, a, j, half):
        return remote(
            piece(j, half), piece(j, half), wy_send.at[way, k, a - 1], wy_recv.at[way, k, a - 1],
            device_id={"groups": lax.rem(g + a, G)},
        )

    def weights_step(k):
        @pl.when(me - 1 - k >= 0)
        def _():
            right(k, me - 1 - k).wait_recv()
            for a in range(1, G):
                across(0, k, a, me - 1 - k, g).start()
            if k + 1 <= C - 2:
                pl.when(me < C - 1)(lambda: right(k + 1, me - 1 - k).start())

        @pl.when(me + 1 + k <= C - 1)
        def _():
            left(k, me + 1 + k).wait_recv()
            for a in range(1, G):
                across(1, k, a, me + 1 + k, g).start()
            if k + 1 <= C - 2:
                pl.when(me > 0)(lambda: left(k + 1, me + 1 + k).start())

    def weights_end(k):
        @pl.when((me - k >= 0) & (me < C - 1))
        def _():
            right(k, me - k).wait_send()

        @pl.when((me + k <= C - 1) & (me > 0))
        def _():
            left(k, me + k).wait_send()

        for way, j, there in ((0, me - 1 - k, me - 1 - k >= 0), (1, me + 1 + k, me + 1 + k <= C - 1)):
            @pl.when(there)
            def _():
                for a in range(1, G):
                    across(way, k, a, j, g).wait_send()
                    across(way, k, a, j, lax.rem(g - a + G, G)).wait_recv()

    def state(q):
        return remote(
            outgoing.at[q], prior.at[q], st_send.at[q], st_recv.at[q], device_id={"ctx": me + 1}
        )

    def block(a, b, q):
        return (lax.rem(h + H - a, H) * S + lax.rem(s + S - b, S)) * K + q

    def gate_x(b, q, blk):
        return remote(
            gates.at[blk], gates.at[blk], gx_send.at[b - 1, q], gx_recv.at[b - 1, q],
            device_id={"state": lax.rem(s + b, S)},
        )

    def gate_core(a, b, q, blk):
        return remote(
            gates.at[blk], gates.at[blk], gc_send.at[a - 1, b, q], gc_recv.at[a - 1, b, q],
            device_id={"head": lax.rem(h + a, H)},
        )

    def square(i, slot):
        a, b = others[i]
        return remote(
            squares.at[slot], squares.at[slot], sq_send.at[i], sq_recv.at[i],
            device_id={"head": lax.rem(h + a, H), "state": lax.rem(s + b, S)},
        )

    w_all[pl.ds(pl.multiple_of(me * rows, rows), rows)] = w_ref[...]

    pl.when(me < C - 1)(lambda: right(0, me).start())
    pl.when(me > 0)(lambda: left(0, me).start())

    @pl.when(me == 0)
    def _():
        prior[...] = jnp.zeros_like(prior)

    summed = jnp.zeros((tokens, 1), f32)
    for q in range(K):
        cols = slice(q * cw, (q + 1) * cw)
        pl.when(me > 0)(lambda: state(q).wait_recv())

        @pl.when(me < C - 1)
        def _():
            outgoing[q] = (
                factor_ref[:, cols] * prior[q].astype(f32) + final_ref[:, cols]
            ).astype(bf16)
            state(q).start()

        own = block(0, 0, q)
        parts = []
        for k in range(spans):
            t = slice(k * SPAN, (k + 1) * SPAN)
            there = reach_ref[k : k + 1, cols] * prior[q].astype(f32)
            if k > 0:
                there = there + entering_ref[k - 1, :, cols]
            inter = jnp.dot(c_ref[t, :], there.astype(bf16), preferred_element_type=f32)
            mixed = base_ref[t, cols] + grow_ref[t, cols] * inter
            z = z_ref[t, cols].astype(f32)
            gated = mixed * (z / (1.0 + jnp.exp(-z)))
            parts.append(jnp.sum(gated * gated, axis=1, keepdims=True))
            gates[own, t, :] = (gated * gain_ref[:, cols]).astype(bf16)
        summed = summed + jnp.concatenate(parts, axis=0)
        for b in range(1, S):
            gate_x(b, q, own).start()
        for a in range(1, H):
            gate_core(a, 0, q, own).start()
        if 1 <= q <= C - 1:
            weights_step(q - 1)
    here = h * S + s
    squares[here] = jnp.broadcast_to(summed, (tokens, 128)).T[:8]
    for i in range(len(others)):
        square(i, here).start()
    for k in range(min(K - 1, C - 1), C - 1):
        weights_step(k)
    for q in range(K):
        for b in range(1, S):
            gate_x(b, q, block(0, b, q)).wait_recv()
            for a in range(1, H):
                gate_core(a, b, q, block(0, b, q)).start()
    for q in range(K):
        for a in range(1, H):
            for b in range(S):
                gate_core(a, b, q, block(a, b, q)).wait_recv()
    for k in range(C - 1):
        weights_end(k)
    for i, (a, b) in enumerate(others):
        square(i, block(a, b, 0) // K).wait_recv()
    mean = jnp.sum(squares[...], axis=0)[:1] / (S * H * K * cw)
    scale = lax.rsqrt(jnp.broadcast_to(mean + 1e-05, (128, tokens)).T[:, :1])
    total[...] = jnp.zeros_like(total)

    @pl.loop(0, S * H * K)
    def _(blk):
        total[...] += jnp.dot(
            gates[blk], w_all[pl.ds(pl.multiple_of(blk * cw, cw), cw)], preferred_element_type=f32
        )

    o_ref[...] = (total[...] * scale).astype(bf16)
    pl.when(me < C - 1)(lambda: [state(q).wait_send() for q in range(K)] and None)
    for q in range(K):
        for b in range(1, S):
            gate_x(b, q, block(0, 0, q)).wait_send()
        for a in range(1, H):
            for b in range(S):
                gate_core(a, b, q, block(0, b, q)).wait_send()
    for i in range(len(others)):
        square(i, here).wait_send()


def finish(axes, w, final, factor, reach, entering, c, base, grow, z, gain):
    G, C, S, H = axes
    bf16, f32 = jnp.bfloat16, jnp.float32
    nstate, width = final.shape
    tokens = c.shape[0]
    cw = min(CHUNK, width)
    K = width // cw
    dma = pltpu.SemaphoreType.DMA
    args = (w, final, factor, reach, entering, c, base, grow, z, gain)
    return pl.pallas_call(
        functools.partial(kernel, axes),
        out_shape=jax.ShapeDtypeStruct((tokens, w.shape[1]), bf16),
        in_specs=[pl.BlockSpec(memory_space=pltpu.VMEM)] * len(args),
        out_specs=pl.BlockSpec(memory_space=pltpu.VMEM),
        scratch_shapes=[
            pltpu.VMEM((C * w.shape[0], w.shape[1]), bf16),
            pltpu.VMEM((K, nstate, cw), bf16),
            pltpu.VMEM((K, nstate, cw), bf16),
            pltpu.VMEM((S * H * K, tokens, cw), bf16),
            pltpu.VMEM((S * H, 8, tokens), f32),
            pltpu.VMEM((tokens, w.shape[1]), f32),
            dma((C - 1,)), dma((C - 1,)), dma((C - 1,)), dma((C - 1,)),
            dma((2, C - 1, G - 1)), dma((2, C - 1, G - 1)), dma((K,)), dma((K,)),
            dma((S - 1, K)), dma((S - 1, K)), dma((H - 1, S, K)), dma((H - 1, S, K)),
            dma((S * H - 1,)), dma((S * H - 1,)),
        ],
        compiler_params=pltpu.CompilerParams(
            collective_id=0, has_side_effects=True, vmem_limit_bytes=60 * 2**20
        ),
    )(*args)


def local(
    x_in, b_in, c_in, z_in, dt_raw, decay_rate, d_skip, conv_x, conv_b, conv_c, norm_gain, w_out
):
    f32, bf16 = jnp.float32, jnp.bfloat16
    parts = lax.axis_size("state")
    part = lax.axis_index("state")
    ctx = lax.axis_size("ctx")
    groups = lax.axis_size("groups")
    tokens = x_in.shape[0]
    heads = dt_raw.shape[1] // parts
    width = x_in.shape[1] // parts
    size = width // heads
    nb = b_in.shape[1]
    taps = conv_x.shape[0]
    spans = tokens // SPAN
    own = lambda a, axis: lax.dynamic_slice_in_dim(
        a, part * (a.shape[axis] // parts), a.shape[axis] // parts, axis
    )
    x_own, dt_own, rate, skip, taps_x = (
        own(x_in, 1), own(dt_raw, 1), own(decay_rate, 0), own(d_skip, 0), own(conv_x, 1)
    )
    rim = tokens - (taps - 1)
    packed = jnp.concatenate([x_own[rim:], b_in[rim:], c_in[rim:]], axis=1)
    onward = [(i, i + 1) for i in range(ctx - 1)]
    arrived = lax.ppermute(packed, "ctx", onward)
    bc = conv_silu(
        jnp.concatenate([b_in, c_in], axis=1),
        arrived[:, width:],
        jnp.concatenate([conv_b, conv_c], axis=1),
    )
    bc_all = lax.all_gather(bc, "state", axis=0)
    x_conv = conv_silu(x_own, arrived[:, :width], taps_x)
    b = jnp.concatenate([bc_all[i, :, :nb] for i in range(parts)], axis=1)
    c = jnp.concatenate([bc_all[i, :, nb:] for i in range(parts)], axis=1)
    b = b.reshape(spans, SPAN, parts * nb)
    c = c.reshape(spans, SPAN, parts * nb)
    step = jax.nn.softplus(dt_own).reshape(spans, SPAN, heads)
    causal = jnp.arange(SPAN)[:, None] >= jnp.arange(SPAN)[None, :]
    cum = jnp.einsum(
        "ts,ksh->kth", causal.astype(f32), -rate * step, precision=lax.Precision.HIGHEST
    )
    last = cum[:, -1, :]
    x_heads = x_conv.reshape(spans, SPAN, heads, size).astype(f32)
    weighted = ((jnp.exp(last[:, None, :] - cum) * step)[..., None] * x_heads).astype(bf16)
    wide = lambda v: jnp.repeat(v, size, axis=-1)
    weighted = weighted.reshape(spans, SPAN, width)
    update = jnp.einsum("ktn,ktm->knm", b, weighted, preferred_element_type=f32)
    running = update[0]
    gain = jnp.exp(last[0])
    entering, reach = [], [jnp.ones_like(gain)]
    for k in range(1, spans):
        entering.append(running)
        reach.append(gain)
        decay = jnp.exp(last[k])
        running = wide(decay) * running + update[k]
        gain = gain * decay
    inner = jnp.einsum("ktn,ksn->kts", c, b, preferred_element_type=f32)
    cum_heads = jnp.transpose(cum, (0, 2, 1))
    gap = cum_heads[:, :, :, None] - cum_heads[:, :, None, :]
    scores = (inner[:, None] * jnp.exp(jnp.where(causal, gap, -jnp.inf))).astype(bf16)
    inputs = (step[..., None] * x_heads).astype(bf16)
    intra = jnp.einsum("khts,kshp->kthp", scores, inputs, preferred_element_type=f32)
    base = (intra + skip[:, None] * x_heads).reshape(tokens, width)
    return finish(
        (groups, ctx, parts, lax.axis_size("head")),
        w_out,
        running,
        wide(gain)[None],
        wide(jnp.stack(reach)),
        jnp.stack(entering),
        c.reshape(tokens, -1),
        base,
        wide(jnp.exp(cum)).reshape(tokens, width),
        z_in,
        norm_gain[None],
    )


def solution(mesh):
    return jax.shard_map(
        local,
        mesh=mesh,
        in_specs=(
            P(("groups", "ctx"), "head"),
            P(("groups", "ctx"), "state"),
            P(("groups", "ctx"), "state"),
            P(("groups", "ctx"), ("head", "state")),
            P(("groups", "ctx"), "head"),
            P("head"),
            P("head"),
            P(None, "head"),
            P(None, "state"),
            P(None, "state"),
            P(("head", "state")),
            P("ctx", ("state", "head")),
        ),
        out_specs=P(("groups", "ctx"), ("state", "head")),
        check_vma=False,
    )
```

time: 356 us -> 268 us (0.75); the launches traced: 351 us -> 268 us
  waiting for transfers between devices: 251 us -> 15 us
  Pallas kernels: 0 us -> 176 us
  local copies, waits for them, and re-layouts: 24 us -> 39.8 us
  other arithmetic: 29.3 us -> 14.9 us
  matrix products: 17.4 us -> 7.3 us
  starting transfers between devices: 9.3 us -> 1.29 us
  blocking collectives: 5.89 us -> 0 us
    pallas_call x0 -> x1, Pallas kernels: none -> 176 us  [finish(): pl.pallas_call(functools.partial(kernel, axes), out_shape=jax.ShapeDtypeS...]
    all_gather x2 -> x0, waiting for transfers between devices: 152 us -> none  [the longest x1 126 us: local(): w_all = lax.all_gather(w_half, ('ctx', 'groups'), axis=0, tiled=True)]
    ppermute x6 -> x0, waiting for transfers between devices: 62.9 us -> none  [local(): got = lax.ppermute(send, 'ctx', onward)]
    ppermute x1, waiting for transfers between devices: 13.6 us -> 0.54 us  [local(): arrived = lax.ppermute(packed, 'ctx', onward)]
    dot_general x3 -> x1, matrix products: 13 us -> 1.29 us  [local(): update = jnp.einsum('ktn,ktm->knm', b, weighted, preferred_element_type=f32)]
    reshape x0 -> x4, local copies, waits for them, and re-layouts: none -> 10.5 us  [the longest x2 9.78 us: local(): base = (intra + skip[:, None] * x_heads).reshape(tokens, width)]
    all_gather x1, waiting for transfers between devices: 22.5 us -> 14.4 us  [local(): bc_all = lax.all_gather(bc, 'state', axis=0)]
    ppermute x6 -> x0, starting transfers between devices: 7.92 us -> none  [local(): got = lax.ppermute(send, 'ctx', onward)]
  transfers between devices with their start and end apart: 10 -> 2, of which waited for: 10 -> 2; matrix products, arithmetic and copies ran while one was open for 6% -> 9% of each run, Pallas kernels for 0% -> 0%
where the time goes in v2:
time: 268 us
  Pallas kernels  176 us (66%)
  local copies, waits for them, and re-layouts  39.8 us (15%)
  waiting for transfers between devices  15 us (6%)
  other arithmetic  14.9 us (6%)
  between operations  13.6 us (5%)
  matrix products  7.3 us (3%)
    pallas_call x1, Pallas kernels, finish(): pl.pallas_call(functools.partial(kernel, axes), out_shape=jax.ShapeDtypeS...  176 us
    all_gather x1, waiting for transfers between devices, local(): bc_all = lax.all_gather(bc, 'state', axis=0)  14.4 us
    reshape x2, local copies, waits for them, and re-layouts, local(): base = (intra + skip[:, None] * x_heads).reshape(tokens, width)  9.78 us
    convert_element_type x3, local copies, waits for them, and re-layouts, local(): x_heads = x_conv.reshape(spans, SPAN, heads, size).astype(f32)  7.25 us
  transfers between devices with their start and end apart: 2, of which 2 were waited for; matrix products, arithmetic and copies ran while one was open for 9% of the time, Pallas kernels for 0%

profile of v2, /device:TPU:26, one launch (start us, length us, event | category | flops | bytes accessed | tf_op | source)
XLA Modules:
  0.0 267.5 jit_solution(7954733571489560976)
XLA Ops:
  6.5 0.7 slice.97
  7.2 0.7 slice.98
  7.9 0.8 dynamic-slice
  8.8 1.3 collective-permute-start
  10.8 0.8 compare_select_fusion
  11.6 0.7 dynamic-slice_negate_fusion
  12.3 0.7 constant_dynamic-update-slice_fusion
  13.1 0.7 dynamic_slice.19
  14.4 1.5 maximum_convert_fusion
  15.9 2.2 multiply_convert_fusion.4
  19.8 2.0 copy.43.grow_ref
  23.5 1.3 constant_dynamic-slice_fusion.1
  25.1 1.2 fusion.19
  26.4 1.9 copy.36
  28.2 3.5 %reshape.56 = f32[2,256,16,64]{1,0,3,2:T(2,128)} reshape(f32[512,1024]{0,1:T(8,128)} %copy.36) | data formatting | bytes 4194304 | tf_op jit(solution)/shard_map/convert_element_type | solution.py:288
  31.8 1.8 copy.34
  33.6 1.9 fusion.13
  35.8 1.9 multiply_convert_fusion.2
  37.7 14.4 %all-gather.3.cloned.1.call-done = bf16[1024,1024]{1,0:T(8,128)(2,1)} async-done(((bf16[512,1024]{1,0:T(8,128)(2,1)}), bf16[1024,1024]{1,0:T(8,128)(2,1)}) %all-gather.3.cloned.1.call-update) | async-done | bytes 2097168 | tf_op jit(solution)/shard_map/all_gather | solution.py:276
  52.1 3.3 %fusion.29 = (bf16[1,512,512]{2,1,0:T(8,128)(2,1)}, bf16[512,512]{1,0:T(8,128)(2,1)}, bf16[512,512]{1,0:T(8,128)(2,1)}, bf16[1,512,512]{2,1,0:T(8,128)(2,1)}, bf...) fusion(bf16[2,512,1024]{2,1,0:T(8,128)(2,1)} %bitcast.60), kind=kLoop, calls=%fused_computation.66 | loop fusion | bytes 5242880 | tf_op jit(solution)/shard_map/slice | solution.py:279
  55.4 2.1 copy.31
  57.5 2.1 copy.32
  59.5 2.0 fusion.14
  61.6 3.7 %bitcast_add_fusion = f32[2,256,16,64]{1,3,2,0:T(8,128)} fusion(f32[2,256,16,64]{1,0,3,2:T(2,128)S(1)} %copy-done, f32[2,16,256]{2,1,0:T(8,128)S(1)} %fusion.21, f32[2,256,256]{2,1,0:T(8,128)S(1)} %fusion.14, pred[256,256]{1,0:T(8,128)(4,1)S(1)} %iota_compare_fusion, bf16[2,256,16,64]{1,0,3,2:T(2,128)(2,1)S(1)} %copy-done.5, f32[16]{0:T(128)S(1)} %dynamic_slice.19), kind=kOutput, calls=%fused_computation.24 | convolution fusion | flops 277872640 | bytes 5865536 | tf_op jit(solution)/shard_map/khts,kshp->kthp/dot_general | solution.py:307
  65.3 4.8 %copy.46 = f32[2,256,16,64]{3,2,1,0:T(8,128)} copy(f32[2,256,16,64]{1,3,2,0:T(8,128)} %bitcast_add_fusion) | data formatting | bytes 4194304 | tf_op jit(solution)/shard_map/reshape | solution.py:308
  70.1 4.9 %reshape.59.base_ref = f32[512,1024]{1,0:T(8,128)} reshape(f32[2,256,16,64]{3,2,1,0:T(8,128)} %copy.46) | data formatting | bytes 4194304 | tf_op jit(solution)/shard_map/reshape | solution.py:308
  75.1 1.3 fusion.20
  76.4 2.3 slice.142.entering_ref
  78.7 2.9 %fusion.1.final_ref = f32[1024,1024]{1,0:T(8,128)} fusion(f32[2,1024,1024]{2,1,0:T(8,128)S(1)} %fusion.20, f32[1024]{0:T(1024)S(1)} %mul.158), kind=kLoop, calls=%fused_computation.3 | loop fusion | flops 2097152 | bytes 12587008 | tf_op jit(solution)/shard_map/add | solution.py:300
  81.6 1.1 pad_maximum_fusion.1.c_ref
  82.7 175.7 %shard_map.118 = bf16[512,1024]{1,0:T(8,128)(2,1)} custom-call(bf16[1024,1024]{1,0:T(8,128)(2,1)} %w_ref.1, f32[1024,1024]{1,0:T(8,128)} %fusion.1.final_ref, f32[1,1024]{1,0:T(1,128)} %broadcast_in_dim_reshape.2.factor_ref, f32[2,1024]{1,0:T(2,128)} %reshape.53.reach_ref, f32[1,1024,1024]{2,1,0:T(8,128)} %slice.142.entering_ref, ...), custom_call_target="tpu_custom_call" | custom-call | tf_op jit(solution)/shard_map/pallas_call | solution.py:223
  258.4 2.3 copy.60
  (41 shorter events, 5.2 us)
Async XLA Ops:
  6.5 45.6 %all-gather.3.cloned.1.call-start = ((), (), s32[]{:S(2)}) async-start(), calls=%async_computation | async-start | bytes 3145728 | tf_op jit(solution)/shard_map/all_gather | solution.py:276
  8.8 5.6 %collective-permute-start = (bf16[3,2048]{1,0:T(4,128)(2,1)S(1)}, bf16[3,2048]{1,0:T(4,128)(2,1)S(1)}, u32[]{:S(2)}, u32[]{:S(2)}) collective-permute-start(bf16[3,2048]{1,0:T(4,128)(2,1)S(1)} %pad_maximum_fusion.4), channel_id=1, source_target_pairs={{0,4},{4,8},{8,12},{1,5},{5,9},{9,13},{2,6},{6,10},{10,14},{3,7},{... | collective-permute-start | bytes 36872 | tf_op jit(solution)/shard_map/ppermute | solution.py:270
  19.8 3.6 %copy-start.6 = (f32[4,2048]{1,0:T(4,128)S(1)}, f32[4,2048]{1,0:T(4,128)}, u32[]{:S(2)}) copy-start(f32[4,2048]{1,0:T(4,128)} %param.19) | copy-start | bytes 98308
  33.6 2.2 copy-start
  59.5 2.0 copy-start.5
  70.1 5.0 %copy-start.1 = (bf16[2,256,512]{1,2,0:T(8,128)(2,1)S(1)}, bf16[2,256,512]{1,2,0:T(8,128)(2,1)}, u32[]{:S(2)}) copy-start(bf16[2,256,512]{1,2,0:T(8,128)(2,1)} %copy.31) | copy-start | bytes 1572868
  70.1 5.0 %copy-start.2 = (bf16[2,256,512]{1,2,0:T(8,128)(2,1)S(1)}, bf16[2,256,512]{1,2,0:T(8,128)(2,1)}, u32[]{:S(2)}) copy-start(bf16[2,256,512]{1,2,0:T(8,128)(2,1)} %copy.32) | copy-start | bytes 1572868
  78.7 2.9 %copy-start.3 = (bf16[512,512]{1,0:T(8,128)(2,1)S(1)}, bf16[512,512]{1,0:T(8,128)(2,1)}, u32[]{:S(2)}) copy-start(bf16[512,512]{1,0:T(8,128)(2,1)} %get-tuple-element.8) | copy-start | bytes 1572868
  78.7 2.9 %copy-start.4 = (bf16[512,512]{1,0:T(8,128)(2,1)S(1)}, bf16[512,512]{1,0:T(8,128)(2,1)}, u32[]{:S(2)}) copy-start(bf16[512,512]{1,0:T(8,128)(2,1)} %get-tuple-element.9) | copy-start | bytes 1572868
Sparse Core Ops, SparseCore 0:
  18.3 33.8 all-gather.2

commit v3 on v2

--- a/solution.py
+++ b/solution.py
@@ -9,21 +9,14 @@
 
 SPAN = 256
 CHUNK = 256
-
-
-def conv_silu(signal, before, weights):
-    length = signal.shape[0]
-    taps = weights.shape[0]
-    joined = jnp.concatenate([before, signal], axis=0).astype(jnp.float32)
-    summed = weights[taps - 1] * joined[taps - 1 :]
-    for k in range(taps - 1):
-        summed = summed + weights[k] * joined[k : k + length]
-    return jax.nn.silu(summed).astype(jnp.bfloat16)
+LANES = 128
+RIM = 16
 
 
 def kernel(
-    axes, w_ref, final_ref, factor_ref, reach_ref, entering_ref, c_ref, base_ref, grow_ref, z_ref,
-    gain_ref, o_ref, w_all, prior, outgoing, gates, squares, total,
+    axes, w_ref, x_ref, b_ref, c_ref, z_ref, stepw_ref, cumw_ref, cum_ref, cumt_ref, skip_ref,
+    tx_ref, tb_ref, tc_ref, gain_ref, o_ref, w_all, prior, outgoing, gates, squares, total,
+    rims, joined, x_conv, bc, inner, rim_send, rim_recv, bx_send, bx_recv, bh_send, bh_recv,
     wr_send, wr_recv, wl_send, wl_recv, wy_send, wy_recv, st_send, st_recv,
     gx_send, gx_recv, gc_send, gc_recv, sq_send, sq_recv,
 ):
@@ -33,7 +26,9 @@
     rows = w_ref.shape[0]
     part = rows // G
     K, nstate, cw = prior.shape
-    tokens = c_ref.shape[0]
+    tokens, nb = c_ref.shape
+    width = x_ref.shape[1]
+    size = width // cum_ref.shape[1]
     spans = tokens // SPAN
     remote = functools.partial(
         pltpu.make_async_remote_copy, device_id_type=pl.DeviceIdType.MESH
@@ -129,6 +124,28 @@
             device_id={"head": lax.rem(h + a, H), "state": lax.rem(s + b, S)},
         )
 
+    def rim(i):
+        ref, at = ((x_ref, 0), (b_ref, width), (c_ref, width + nb))[i]
+        return remote(
+            ref.at[pl.ds(tokens - RIM, RIM)], rims.at[:, pl.ds(at, ref.shape[1])],
+            rim_send.at[i], rim_recv.at[i], device_id={"ctx": me + 1},
+        )
+
+    def half_x(b):
+        return remote(
+            bc.at[h, s], bc.at[h, s], bx_send.at[b - 1], bx_recv.at[b - 1],
+            device_id={"state": lax.rem(s + b, S)},
+        )
+
+    def half_core(b, which):
+        there = lax.rem(s + S - b, S)
+        return remote(
+            bc.at[which, there], bc.at[which, there], bh_send.at[b - 1], bh_recv.at[b - 1],
+            device_id={"head": 1 - h},
+        )
+
+    for i in range(3):
+        pl.when(me < C - 1)(lambda: rim(i).start())
     w_all[pl.ds(pl.multiple_of(me * rows, rows), rows)] = w_ref[...]
 
     pl.when(me < C - 1)(lambda: right(0, me).start())
@@ -137,28 +154,102 @@
     @pl.when(me == 0)
     def _():
         prior[...] = jnp.zeros_like(prior)
+        rims[...] = jnp.zeros_like(rims)
+
+    for i in range(3):
+        pl.when(me > 0)(lambda: rim(i).wait_recv())
+
+    def conv(ref, taps_ref, at):
+        wide = ref.shape[1]
+        joined[:RIM, :wide] = rims[:, at : at + wide].astype(f32)
+        joined[RIM:, :wide] = ref[...].astype(f32)
+        taps = taps_ref.shape[0]
+        v = jnp.zeros((tokens, wide), f32)
+        for k in range(taps):
+            v = v + taps_ref[k : k + 1, :] * joined[pl.ds(RIM - taps + 1 + k, tokens), :wide]
+        return (v / (1.0 + jnp.exp(-v))).astype(bf16)
+
+    bc[0, s] = conv(b_ref, tb_ref, width)
+    bc[1, s] = conv(c_ref, tc_ref, width + nb)
+    for b in range(1, S):
+        half_x(b).start()
+    x_conv[...] = conv(x_ref, tx_ref, 0)
+    for b in range(1, S):
+        half_x(b).wait_recv()
+        half_core(b, h).start()
+    for b in range(1, S):
+        half_core(b, 1 - h).wait_recv()
+    causal = lax.broadcasted_iota(jnp.int32, (SPAN, SPAN), 0) >= lax.broadcasted_iota(
+        jnp.int32, (SPAN, SPAN), 1
+    )
+    lane = lax.broadcasted_iota(jnp.int32, (SPAN, LANES), 1) // size
+    for k in range(spans):
+        t = slice(k * SPAN, (k + 1) * SPAN)
+        inner[k] = sum(
+            lax.dot_general(
+                bc[1, b, t, :], bc[0, b, t, :], (((1,), (1,)), ((), ())), preferred_element_type=f32
+            )
+            for b in range(S)
+        )
 
     summed = jnp.zeros((tokens, 1), f32)
     for q in range(K):
         cols = slice(q * cw, (q + 1) * cw)
+        running = jnp.zeros((nstate, cw), f32)
+        reach = jnp.ones((1, cw), f32)
+        before = []
+        for k in range(spans):
+            t = slice(k * SPAN, (k + 1) * SPAN)
+            before.append((reach, running))
+            last = cumw_ref[(k + 1) * SPAN - 1 : (k + 1) * SPAN, cols]
+            weighted = (
+                jnp.exp(last - cumw_ref[t, cols]) * stepw_ref[t, cols] * x_conv[t, cols].astype(f32)
+            ).astype(bf16)
+            update = jnp.concatenate(
+                [
+                    lax.dot_general(
+                        bc[0, b, t, :], weighted, (((0,), (0,)), ((), ())), preferred_element_type=f32
+                    )
+                    for b in range(S)
+                ],
+                axis=0,
+            )
+            decay = jnp.exp(last)
+            running = decay * running + update
+            reach = reach * decay
         pl.when(me > 0)(lambda: state(q).wait_recv())
 
         @pl.when(me < C - 1)
         def _():
-            outgoing[q] = (
-                factor_ref[:, cols] * prior[q].astype(f32) + final_ref[:, cols]
-            ).astype(bf16)
+            outgoing[q] = (reach * prior[q].astype(f32) + running).astype(bf16)
             state(q).start()
 
         own = block(0, 0, q)
         parts = []
         for k in range(spans):
             t = slice(k * SPAN, (k + 1) * SPAN)
-            there = reach_ref[k : k + 1, cols] * prior[q].astype(f32)
-            if k > 0:
-                there = there + entering_ref[k - 1, :, cols]
-            inter = jnp.dot(c_ref[t, :], there.astype(bf16), preferred_element_type=f32)
-            mixed = base_ref[t, cols] + grow_ref[t, cols] * inter
+            x = x_conv[t, cols].astype(f32)
+            inputs = (stepw_ref[t, cols] * x).astype(bf16)
+            intra = []
+            for p in range(cw // LANES):
+                piece_in = inputs[:, p * LANES : (p + 1) * LANES]
+                got = jnp.zeros((SPAN, LANES), f32)
+                for i in range(LANES // size):
+                    head = (q * cw + p * LANES) // size + i
+                    gap = cum_ref[t, head : head + 1] - cumt_ref[head : head + 1, t]
+                    scores = (inner[k] * jnp.exp(jnp.where(causal, gap, -jnp.inf))).astype(bf16)
+                    one = jnp.dot(scores, piece_in, preferred_element_type=f32)
+                    got = jnp.where(lane == i, one, got)
+                intra.append(got)
+            there = (before[k][0] * prior[q].astype(f32) + before[k][1]).astype(bf16)
+            inter = sum(
+                jnp.dot(bc[1, b, t, :], there[b * nb : (b + 1) * nb], preferred_element_type=f32)
+                for b in range(S)
+            )
+            mixed = (
+                jnp.concatenate(intra, axis=1) + skip_ref[:, cols] * x
+                + jnp.exp(cumw_ref[t, cols]) * inter
+            )
             z = z_ref[t, cols].astype(f32)
             gated = mixed * (z / (1.0 + jnp.exp(-z)))
             parts.append(jnp.sum(gated * gated, axis=1, keepdims=True))
@@ -168,13 +259,13 @@
             gate_x(b, q, own).start()
         for a in range(1, H):
             gate_core(a, 0, q, own).start()
-        if 1 <= q <= C - 1:
-            weights_step(q - 1)
+        if q < C - 1:
+            weights_step(q)
     here = h * S + s
     squares[here] = jnp.broadcast_to(summed, (tokens, 128)).T[:8]
     for i in range(len(others)):
         square(i, here).start()
-    for k in range(min(K - 1, C - 1), C - 1):
+    for k in range(min(K, C - 1), C - 1):
         weights_step(k)
     for q in range(K):
         for b in range(1, S):
@@ -209,17 +300,23 @@
                 gate_core(a, b, q, block(0, b, q)).wait_send()
     for i in range(len(others)):
         square(i, here).wait_send()
-
-
-def finish(axes, w, final, factor, reach, entering, c, base, grow, z, gain):
+    for i in range(3):
+        pl.when(me < C - 1)(lambda: rim(i).wait_send())
+    for b in range(1, S):
+        half_x(b).wait_send()
+        half_core(b, h).wait_send()
+
+
+def finish(axes, *args):
     G, C, S, H = axes
     bf16, f32 = jnp.bfloat16, jnp.float32
-    nstate, width = final.shape
-    tokens = c.shape[0]
+    w, x, b = args[:3]
+    tokens, width = x.shape
+    nb = b.shape[1]
+    nstate = nb * S
     cw = min(CHUNK, width)
     K = width // cw
     dma = pltpu.SemaphoreType.DMA
-    args = (w, final, factor, reach, entering, c, base, grow, z, gain)
     return pl.pallas_call(
         functools.partial(kernel, axes),
         out_shape=jax.ShapeDtypeStruct((tokens, w.shape[1]), bf16),
@@ -232,6 +329,12 @@
             pltpu.VMEM((S * H * K, tokens, cw), bf16),
             pltpu.VMEM((S * H, 8, tokens), f32),
             pltpu.VMEM((tokens, w.shape[1]), f32),
+            pltpu.VMEM((RIM, width + 2 * nb), bf16),
+            pltpu.VMEM((tokens + RIM, max(width, nb)), f32),
+            pltpu.VMEM((tokens, width), bf16),
+            pltpu.VMEM((2, S, tokens, nb), bf16),
+            pltpu.VMEM((tokens // SPAN, SPAN, SPAN), f32),
+            dma((3,)), dma((3,)), dma((S - 1,)), dma((S - 1,)), dma((S - 1,)), dma((S - 1,)),
             dma((C - 1,)), dma((C - 1,)), dma((C - 1,)), dma((C - 1,)),
             dma((2, C - 1, G - 1)), dma((2, C - 1, G - 1)), dma((K,)), dma((K,)),
             dma((S - 1, K)), dma((S - 1, K)), dma((H - 1, S, K)), dma((H - 1, S, K)),
@@ -246,7 +349,7 @@
 def local(
     x_in, b_in, c_in, z_in, dt_raw, decay_rate, d_skip, conv_x, conv_b, conv_c, norm_gain, w_out
 ):
-    f32, bf16 = jnp.float32, jnp.bfloat16
+    f32 = jnp.float32
     parts = lax.axis_size("state")
     part = lax.axis_index("state")
     ctx = lax.axis_size("ctx")
@@ -255,8 +358,6 @@
     heads = dt_raw.shape[1] // parts
     width = x_in.shape[1] // parts
     size = width // heads
-    nb = b_in.shape[1]
-    taps = conv_x.shape[0]
     spans = tokens // SPAN
     own = lambda a, axis: lax.dynamic_slice_in_dim(
         a, part * (a.shape[axis] // parts), a.shape[axis] // parts, axis
@@ -264,59 +365,30 @@
     x_own, dt_own, rate, skip, taps_x = (
         own(x_in, 1), own(dt_raw, 1), own(decay_rate, 0), own(d_skip, 0), own(conv_x, 1)
     )
-    rim = tokens - (taps - 1)
-    packed = jnp.concatenate([x_own[rim:], b_in[rim:], c_in[rim:]], axis=1)
-    onward = [(i, i + 1) for i in range(ctx - 1)]
-    arrived = lax.ppermute(packed, "ctx", onward)
-    bc = conv_silu(
-        jnp.concatenate([b_in, c_in], axis=1),
-        arrived[:, width:],
-        jnp.concatenate([conv_b, conv_c], axis=1),
-    )
-    bc_all = lax.all_gather(bc, "state", axis=0)
-    x_conv = conv_silu(x_own, arrived[:, :width], taps_x)
-    b = jnp.concatenate([bc_all[i, :, :nb] for i in range(parts)], axis=1)
-    c = jnp.concatenate([bc_all[i, :, nb:] for i in range(parts)], axis=1)
-    b = b.reshape(spans, SPAN, parts * nb)
-    c = c.reshape(spans, SPAN, parts * nb)
-    step = jax.nn.softplus(dt_own).reshape(spans, SPAN, heads)
+    step = jax.nn.softplus(dt_own)
     causal = jnp.arange(SPAN)[:, None] >= jnp.arange(SPAN)[None, :]
     cum = jnp.einsum(
-        "ts,ksh->kth", causal.astype(f32), -rate * step, precision=lax.Precision.HIGHEST
-    )
-    last = cum[:, -1, :]
-    x_heads = x_conv.reshape(spans, SPAN, heads, size).astype(f32)
-    weighted = ((jnp.exp(last[:, None, :] - cum) * step)[..., None] * x_heads).astype(bf16)
+        "ts,ksh->kth",
+        causal.astype(f32),
+        (-rate * step).reshape(spans, SPAN, heads),
+        precision=lax.Precision.HIGHEST,
+    ).reshape(tokens, heads)
     wide = lambda v: jnp.repeat(v, size, axis=-1)
-    weighted = weighted.reshape(spans, SPAN, width)
-    update = jnp.einsum("ktn,ktm->knm", b, weighted, preferred_element_type=f32)
-    running = update[0]
-    gain = jnp.exp(last[0])
-    entering, reach = [], [jnp.ones_like(gain)]
-    for k in range(1, spans):
-        entering.append(running)
-        reach.append(gain)
-        decay = jnp.exp(last[k])
-        running = wide(decay) * running + update[k]
-        gain = gain * decay
-    inner = jnp.einsum("ktn,ksn->kts", c, b, preferred_element_type=f32)
-    cum_heads = jnp.transpose(cum, (0, 2, 1))
-    gap = cum_heads[:, :, :, None] - cum_heads[:, :, None, :]
-    scores = (inner[:, None] * jnp.exp(jnp.where(causal, gap, -jnp.inf))).astype(bf16)
-    inputs = (step[..., None] * x_heads).astype(bf16)
-    intra = jnp.einsum("khts,kshp->kthp", scores, inputs, preferred_element_type=f32)
-    base = (intra + skip[:, None] * x_heads).reshape(tokens, width)
     return finish(
         (groups, ctx, parts, lax.axis_size("head")),
         w_out,
-        running,
-        wide(gain)[None],
-        wide(jnp.stack(reach)),
-        jnp.stack(entering),
-        c.reshape(tokens, -1),
-        base,
-        wide(jnp.exp(cum)).reshape(tokens, width),
+        x_own,
+        b_in,
+        c_in,
         z_in,
+        wide(step),
+        wide(cum),
+        cum,
+        cum.T,
+        wide(skip)[None],
+        taps_x,
+        conv_b,
+        conv_c,
         norm_gain[None],
     )
 

time: 268 us -> 180 us (0.67)
  local copies, waits for them, and re-layouts: 39.8 us -> 14.6 us
  Pallas kernels: 176 us -> 160 us
  waiting for transfers between devices: 15 us -> 0 us
  between operations: 13.6 us -> 0.04 us
  other arithmetic: 14.9 us -> 1.71 us
  matrix products: 7.3 us -> 0.27 us
    pallas_call x1, Pallas kernels: 176 us -> 160 us  [finish(): pl.pallas_call(functools.partial(kernel, axes), out_shape=jax.ShapeDtypeS...]
    all_gather x1 -> x0, waiting for transfers between devices: 14.4 us -> none  [local(): bc_all = lax.all_gather(bc, 'state', axis=0)]
    convert_element_type x6 -> x0, other arithmetic: 9.1 us -> none  [the longest x1 2.24 us: conv_silu(): return jax.nn.silu(summed).astype(jnp.bfloat16)]
    reshape x3 -> x2, local copies, waits for them, and re-layouts: 9.81 us -> 0.84 us  [local(): cum = jnp.einsum('ts,ksh->kth', causal.astype(f32), (-rate * step).reshap...]
    slice x9 -> x0, local copies, waits for them, and re-layouts: 8.03 us -> none  [the longest x1 3.27 us: local(): c = jnp.concatenate([bc_all[i, :, nb:] for i in range(parts)], axis=1)]
    convert_element_type x3 -> x0, local copies, waits for them, and re-layouts: 7.25 us -> none  [local(): x_heads = x_conv.reshape(spans, SPAN, heads, size).astype(f32)]
    dot_general x4 -> x1, matrix products: 7.3 us -> 0.27 us  [local(): jnp.einsum('ts,ksh->kth', causal.astype(f32), (-rate * step).reshape(span...]
    reshape x1 -> x2, local copies, waits for them, and re-layouts: 0.67 us -> 5.82 us  [local(): wide = lambda v: jnp.repeat(v, size, axis=-1)]
  transfers between devices with their start and end apart: 2 -> 0, of which waited for: 2 -> 0; matrix products, arithmetic and copies ran while one was open for 9% -> 0% of each run, Pallas kernels for 0% -> 0%
where the time goes in v3:
time: 180 us; the launch traced here: 177 us
  Pallas kernels  160 us (89%)
  local copies, waits for them, and re-layouts  14.6 us (8%)
    pallas_call x1, Pallas kernels, finish(): pl.pallas_call(functools.partial(kernel, axes), out_shape=jax.ShapeDtypeS...  160 us
    reshape x2, local copies, waits for them, and re-layouts, local(): wide = lambda v: jnp.repeat(v, size, axis=-1)  5.82 us

profile of v3, /device:TPU:26, one launch (start us, length us, event | category | flops | bytes accessed | tf_op | source)
XLA Modules:
  0.0 176.9 jit_solution(3262551447553046445)
XLA Ops:
  0.0 0.0 copy-start
  0.0 0.9 dynamic-slice_negate_fusion
  0.9 0.8 broadcast_multiply_fusion
  1.7 0.3 convolution_bitcast_fusion
  2.0 0.0 copy-start.1
  2.0 1.6 broadcast_in_dim.16
  3.6 2.9 %copy.21.cumw_ref = f32[512,1024]{1,0:T(8,128)} copy(f32[512,1024]{0,1:T(8,128)} %bitcast.17) | data formatting | bytes 4194304 | tf_op jit(solution)/shard_map/reshape | solution.py:376
  6.5 0.0 copy-done.1
  6.5 0.8 copy.22.cum_ref
  7.3 1.6 broadcast_in_dim.15
  8.9 0.0 copy-start.3
  8.9 2.9 %copy.20.stepw_ref = f32[512,1024]{1,0:T(8,128)} copy(f32[512,1024]{0,1:T(8,128)} %bitcast.16) | data formatting | bytes 4194304 | tf_op jit(solution)/shard_map/reshape | solution.py:376
  11.8 0.0 copy-done.3
  11.8 0.0 copy-start.2
  11.8 0.1 dynamic_slice.18
  11.9 0.1 broadcast_in_dim.17
  12.0 0.7 broadcast_in_dim_reshape.3.skip_ref
  12.7 0.0 copy-done
  12.7 1.1 constant_dynamic-slice_fusion.1.x_ref
  13.7 0.0 copy-done.2
  13.7 0.6 constant_dynamic-slice_fusion.tx_ref
  14.3 160.3 %shard_map.118 = bf16[512,1024]{1,0:T(8,128)(2,1)} custom-call(bf16[1024,1024]{1,0:T(8,128)(2,1)} %w_ref.1, bf16[512,1024]{1,0:T(8,128)(2,1)} %constant_dynamic-slice_fusion.1.x_ref, bf16[512,512]{1,0:T(8,128)(2,1)} %b_ref.1, bf16[512,512]{1,0:T(8,128)(2,1)} %c_ref.1, bf16[512,1024]{1,0:T(8,128)(2,1)} %z_ref.1, f32[512,1024]{1,0:T(8,128)} %copy.20.stepw_ref, ...), custom_call_target="tpu_custom_call" | custom-call | tf_op jit(solution)/shard_map/pallas_call | solution.py:320
  174.7 2.3 %copy.30 = bf16[512,1024]{1,0:T(8,128)(2,1)} copy(bf16[512,1024]{1,0:T(8,128)(2,1)} %shard_map.118) | data formatting | bytes 2097152
  (1 shorter events, 0.0 us)
Async XLA Ops:
  0.0 12.7 %copy-start = (bf16[512,2048]{1,0:T(8,128)(2,1)S(1)}, bf16[512,2048]{1,0:T(8,128)(2,1)}, u32[]{:S(2)}) copy-start(bf16[512,2048]{1,0:T(8,128)(2,1)} %param.12) | copy-start | bytes 6291460
  2.0 4.5 %copy-start.1 = (f32[2,2,8,256]{3,2,0,1:T(8,128)}, f32[2,2,8,256]{3,2,0,1:T(8,128)S(1)}, u32[]{:S(2)}) copy-start(f32[2,2,8,256]{3,2,0,1:T(8,128)S(1)} %copy.24) | copy-start | bytes 98308
  8.9 2.9 %copy-start.3 = (f32[32]{0:T(128)S(1)}, f32[32]{0:T(128)}, u32[]{:S(2)}) copy-start(f32[32]{0:T(128)} %param.18) | copy-start | bytes 388
  11.8 1.9 %copy-start.2 = (f32[4,2048]{1,0:T(4,128)S(1)}, f32[4,2048]{1,0:T(4,128)}, u32[]{:S(2)}) copy-start(f32[4,2048]{1,0:T(4,128)} %param.19) | copy-start | bytes 98308

commit v4 on v3

--- a/solution.py
+++ b/solution.py
@@ -14,9 +14,9 @@
 
 
 def kernel(
-    axes, w_ref, x_ref, b_ref, c_ref, z_ref, stepw_ref, cumw_ref, cum_ref, cumt_ref, skip_ref,
+    axes, w_ref, x_ref, b_ref, c_ref, z_ref, step_ref, cum_ref, cumt_ref, skip_ref,
     tx_ref, tb_ref, tc_ref, gain_ref, o_ref, w_all, prior, outgoing, gates, squares, total,
-    rims, joined, x_conv, bc, inner, rim_send, rim_recv, bx_send, bx_recv, bh_send, bh_recv,
+    rims, joined, x_conv, bc, inner, stepw_ref, cumw_ref, rim_send, rim_recv, bx_send, bx_recv, bh_send, bh_recv,
     wr_send, wr_recv, wl_send, wl_recv, wy_send, wy_recv, st_send, st_recv,
     gx_send, gx_recv, gc_send, gc_recv, sq_send, sq_recv,
 ):
@@ -156,6 +156,15 @@
         prior[...] = jnp.zeros_like(prior)
         rims[...] = jnp.zeros_like(rims)
 
+    heads = cum_ref.shape[1]
+    spread = (
+        lax.broadcasted_iota(jnp.int32, (heads, width), 1) // size
+        == lax.broadcasted_iota(jnp.int32, (heads, width), 0)
+    ).astype(f32)
+    for small, large in ((step_ref, stepw_ref), (cum_ref, cumw_ref)):
+        large[...] = jnp.dot(
+            small[...], spread, precision=lax.Precision.HIGHEST, preferred_element_type=f32
+        )
     for i in range(3):
         pl.when(me > 0)(lambda: rim(i).wait_recv())
 
@@ -177,6 +186,7 @@
     for b in range(1, S):
         half_x(b).wait_recv()
         half_core(b, h).start()
+    weights_step(0)
     for b in range(1, S):
         half_core(b, 1 - h).wait_recv()
     causal = lax.broadcasted_iota(jnp.int32, (SPAN, SPAN), 0) >= lax.broadcasted_iota(
@@ -191,6 +201,12 @@
             )
             for b in range(S)
         )
+
+    def pass_on(q):
+        for b in range(1, S):
+            gate_x(b, q, block(0, b, q)).wait_recv()
+            for a in range(1, H):
+                gate_core(a, b, q, block(0, b, q)).start()
 
     summed = jnp.zeros((tokens, 1), f32)
     for q in range(K):
@@ -259,37 +275,41 @@
             gate_x(b, q, own).start()
         for a in range(1, H):
             gate_core(a, 0, q, own).start()
-        if q < C - 1:
-            weights_step(q)
+        if q + 1 < C - 1:
+            weights_step(q + 1)
+        if q >= 1:
+            pass_on(q - 1)
     here = h * S + s
     squares[here] = jnp.broadcast_to(summed, (tokens, 128)).T[:8]
     for i in range(len(others)):
         square(i, here).start()
-    for k in range(min(K, C - 1), C - 1):
+    for k in range(min(K + 1, C - 1), C - 1):
         weights_step(k)
+    for k in range(C - 1):
+        weights_end(k)
+    tile = min(256, total.shape[1])
     for q in range(K):
-        for b in range(1, S):
-            gate_x(b, q, block(0, b, q)).wait_recv()
-            for a in range(1, H):
-                gate_core(a, b, q, block(0, b, q)).start()
-    for q in range(K):
+        if q == max(K - 2, 0):
+            pass_on(K - 1)
         for a in range(1, H):
             for b in range(S):
                 gate_core(a, b, q, block(a, b, q)).wait_recv()
-    for k in range(C - 1):
-        weights_end(k)
+
+        @pl.loop(0, total.shape[1] // tile)
+        def _(n):
+            cols = pl.ds(pl.multiple_of(n * tile, tile), tile)
+            acc = jnp.zeros((tokens, tile), f32) if q == 0 else total[:, cols]
+            for d in range(S * H):
+                blk = d * K + q
+                acc = acc + jnp.dot(
+                    gates[blk], w_all[blk * cw : (blk + 1) * cw, cols], preferred_element_type=f32
+                )
+            total[:, cols] = acc
+
     for i, (a, b) in enumerate(others):
         square(i, block(a, b, 0) // K).wait_recv()
     mean = jnp.sum(squares[...], axis=0)[:1] / (S * H * K * cw)
     scale = lax.rsqrt(jnp.broadcast_to(mean + 1e-05, (128, tokens)).T[:, :1])
-    total[...] = jnp.zeros_like(total)
-
-    @pl.loop(0, S * H * K)
-    def _(blk):
-        total[...] += jnp.dot(
-            gates[blk], w_all[pl.ds(pl.multiple_of(blk * cw, cw), cw)], preferred_element_type=f32
-        )
-
     o_ref[...] = (total[...] * scale).astype(bf16)
     pl.when(me < C - 1)(lambda: [state(q).wait_send() for q in range(K)] and None)
     for q in range(K):
@@ -334,6 +354,8 @@
             pltpu.VMEM((tokens, width), bf16),
             pltpu.VMEM((2, S, tokens, nb), bf16),
             pltpu.VMEM((tokens // SPAN, SPAN, SPAN), f32),
+            pltpu.VMEM((tokens, width), f32),
+            pltpu.VMEM((tokens, width), f32),
             dma((3,)), dma((3,)), dma((S - 1,)), dma((S - 1,)), dma((S - 1,)), dma((S - 1,)),
             dma((C - 1,)), dma((C - 1,)), dma((C - 1,)), dma((C - 1,)),
             dma((2, C - 1, G - 1)), dma((2, C - 1, G - 1)), dma((K,)), dma((K,)),
@@ -381,8 +403,7 @@
         b_in,
         c_in,
         z_in,
-        wide(step),
-        wide(cum),
+        step,
         cum,
         cum.T,
         wide(skip)[None],

time: 180 us -> 154 us (0.86); the launches traced: 177 us -> 154 us
  Pallas kernels: 160 us -> 144 us
  local copies, waits for them, and re-layouts: 14.6 us -> 7.86 us
    pallas_call x1, Pallas kernels: 160 us -> 144 us  [finish(): pl.pallas_call(functools.partial(kernel, axes), out_shape=jax.ShapeDtypeS...]
    reshape x2 -> x0, local copies, waits for them, and re-layouts: 5.82 us -> none  [local(): wide = lambda v: jnp.repeat(v, size, axis=-1)]
    broadcast_in_dim x3 -> x1, local copies, waits for them, and re-layouts: 3.23 us -> 0.07 us  [local(): wide = lambda v: jnp.repeat(v, size, axis=-1)]
    dynamic_slice x3 -> x4, local copies, waits for them, and re-layouts: 1.74 us -> 3.87 us  [local(): lax.dynamic_slice_in_dim(a, part * (a.shape[axis] // parts), a.shape[axis...]
where the time goes in v4:
time: 154 us
  Pallas kernels  144 us (94%)
  local copies, waits for them, and re-layouts  7.86 us (5%)
  other arithmetic  1.74 us (1%)
    pallas_call x1, Pallas kernels, finish(): pl.pallas_call(functools.partial(kernel, axes), out_shape=jax.ShapeDtypeS...  144 us
    dynamic_slice x4, local copies, waits for them, and re-layouts, local(): lax.dynamic_slice_in_dim(a, part * (a.shape[axis] // parts), a.shape[axis...  3.87 us

profile of v4, /device:TPU:26, one launch (start us, length us, event | category | flops | bytes accessed | tf_op | source)
XLA Modules:
  0.0 154.1 jit_solution(4059950606363344030)
XLA Ops:
  0.0 0.0 copy-start
  0.0 0.9 dynamic-slice_negate_fusion
  0.9 0.7 dynamic_slice.18
  1.6 0.1 broadcast_in_dim.4
  1.7 0.7 broadcast_in_dim_reshape.3.skip_ref
  2.4 1.3 constant_dynamic-slice_fusion.tx_ref
  3.7 0.8 constant_dynamic-slice_fusion.1
  4.4 0.1 copy.18
  4.6 0.9 broadcast_multiply_fusion
  5.4 0.3 convolution_bitcast_fusion
  5.8 0.0 copy-start.1
  5.8 0.8 copy.16.cum_ref
  6.6 0.0 copy-done
  6.6 1.1 constant_dynamic-slice_fusion.2.x_ref
  7.7 0.0 copy-done.1
  7.7 144.1 %shard_map.118 = bf16[512,1024]{1,0:T(8,128)(2,1)} custom-call(bf16[1024,1024]{1,0:T(8,128)(2,1)} %w_ref.1, bf16[512,1024]{1,0:T(8,128)(2,1)} %constant_dynamic-slice_fusion.2.x_ref, bf16[512,512]{1,0:T(8,128)(2,1)} %b_ref.1, bf16[512,512]{1,0:T(8,128)(2,1)} %c_ref.1, bf16[512,1024]{1,0:T(8,128)(2,1)} %z_ref.1, f32[512,16]{1,0:T(8,128)} %get-tuple-element.6.step_ref, ...), custom_call_target="tpu_custom_call" | custom-call | tf_op jit(solution)/shard_map/pallas_call | solution.py:340
  151.9 2.3 %copy.21 = bf16[512,1024]{1,0:T(8,128)(2,1)} copy(bf16[512,1024]{1,0:T(8,128)(2,1)} %shard_map.118) | data formatting | bytes 2097152
  (1 shorter events, 0.0 us)
Async XLA Ops:
  0.0 6.6 %copy-start = (bf16[512,2048]{1,0:T(8,128)(2,1)S(1)}, bf16[512,2048]{1,0:T(8,128)(2,1)}, u32[]{:S(2)}) copy-start(bf16[512,2048]{1,0:T(8,128)(2,1)} %param.12) | copy-start | bytes 6291460
  5.8 1.9 %copy-start.1 = (f32[2,2,8,256]{3,2,0,1:T(8,128)}, f32[2,2,8,256]{3,2,0,1:T(8,128)S(1)}, u32[]{:S(2)}) copy-start(f32[2,2,8,256]{3,2,0,1:T(8,128)S(1)} %copy.19) | copy-start | bytes 98308
